TPU v7x, 256 devices: a whole 4x4x8 slice. The times are simulated.
256 devices in a mesh: freq: 16 (over y, x), stn: 16 (over z, core).
Axes of the slice: x: 4, y: 4, z: 8, core: 2. Of those that a mesh axis runs over, the one named last changes fastest.
Arguments:
- visibilities: float32 [16, 8, 1024, 1024], P('freq', None, 'stn'), may hold values from -6 to 6
- flag_mask: int32 [1024, 1024], P('stn'), may hold values 0 or 1
- stations: float32 [3, 1024], P(None, 'stn'), may hold values from -32 to 32
- directions: float32 [2, 1536], replicated, may hold values from -0.5 to 0.5
- intensity: float32 [1536], replicated, may hold values from 0.02 to 0.2
- polarized: float32 [2, 1536], replicated, may hold values from -0.4375 to 0.4375
- spectral: float32 [1536], replicated, may hold values from -1.5 to 0.5
- clusters: int32 [1536], replicated, may hold values from 0 to 15, as said below
- jones_gains: float32 [16, 8, 16, 1024], P('freq', None, None, 'stn'), may hold values from -6 to 6
- scaled_duals: float32 [16, 8, 16, 1024], P('freq', None, None, 'stn'), may hold values from -4 to 4
- consensus: float32 [4, 8, 16, 1024], P(None, None, None, 'stn'), may hold values from -6 to 6
Outputs:
- jones_next: float32 [16, 8, 16, 1024], P('freq', None, None, 'stn')
- duals_next: float32 [16, 8, 16, 1024], P('freq', None, None, 'stn')
- consensus_next: float32 [4, 8, 16, 1024], P(None, None, None, 'stn')
Inputs may be any that keep to these rules, and one draw needn't show every extreme that they name: `clusters`: every direction holds exactly 96 components.
All inputs are finite; a program needn't handle non-finite values. No bound on the sum of `flag_mask` on one device may be relied on, other than what follows from the above.
Results may differ from a plain program's by a relative error of at most 0.0019.
Values may be sent and summed in bfloat16 or wider, within the bound.
No kernel may reach another device: no remote copies, remote signals or barrier semaphores. Data moves between devices by JAX's collectives and lax.ppermute only.
A program may use at most 64 MiB of HBM per device.

v0:
```python
import jax
import jax.numpy as jnp
from jax import lax
from jax.sharding import PartitionSpec as P

DIRS = 16


TWO_PI = 6.283185307179586
PENALTY = 40.0
STEP_SIZE = 0.5


def complex_mul(lhs_value, rhs_value):
    return (
        lhs_value[0] * rhs_value[0] - lhs_value[1] * rhs_value[1],
        lhs_value[0] * rhs_value[1] + lhs_value[1] * rhs_value[0],
    )


def complex_add(lhs_value, rhs_value):
    return (lhs_value[0] + rhs_value[0], lhs_value[1] + rhs_value[1])


def complex_conj(number):
    return (number[0], -number[1])


def matrix_mul(lhs_matrix, rhs_matrix):
    return [
        complex_add(
            complex_mul(lhs_matrix[0], rhs_matrix[0]), complex_mul(lhs_matrix[1], rhs_matrix[2])
        ),
        complex_add(
            complex_mul(lhs_matrix[0], rhs_matrix[1]), complex_mul(lhs_matrix[1], rhs_matrix[3])
        ),
        complex_add(
            complex_mul(lhs_matrix[2], rhs_matrix[0]), complex_mul(lhs_matrix[3], rhs_matrix[2])
        ),
        complex_add(
            complex_mul(lhs_matrix[2], rhs_matrix[1]), complex_mul(lhs_matrix[3], rhs_matrix[3])
        ),
    ]


def matrix_herm(matrix):
    return [
        complex_conj(matrix[0]),
        complex_conj(matrix[2]),
        complex_conj(matrix[1]),
        complex_conj(matrix[3]),
    ]


def unpack_matrix(stacked):
    return [
        (stacked[0], stacked[1]),
        (stacked[2], stacked[3]),
        (stacked[4], stacked[5]),
        (stacked[6], stacked[7]),
    ]


def pack_matrix(matrix):
    return jnp.stack([member for element in matrix for member in element])


def summed_pack(matrix, reduce_dim):
    return -jnp.stack([jnp.sum(member, reduce_dim) for element in matrix for member in element])


def band_ratio(index_value, band_count):
    return 0.5 + 3.0 * (index_value.astype(jnp.float32) + 0.5) / band_count


def station_table(positions, sky_dirs, freq_ratio):
    dir_l = sky_dirs[0][None, :]
    dir_m = sky_dirs[1][None, :]
    dir_n = jnp.sqrt(1.0 - dir_l * dir_l - dir_m * dir_m)
    geometry = (
        dir_l * positions[0][:, None]
        + dir_m * positions[1][:, None]
        + (dir_n - 1.0) * positions[2][:, None]
    )
    phase_angle = TWO_PI * freq_ratio * geometry
    return jnp.stack([jnp.cos(phase_angle), -jnp.sin(phase_angle)]).astype(jnp.bfloat16)


def flux_weights(intensity, polarized, spectral, freq_ratio):
    factor = jnp.power(freq_ratio, spectral)
    return jnp.stack(
        [
            (intensity + polarized[0]) * factor,
            polarized[1] * factor,
            (intensity - polarized[0]) * factor,
        ]
    )


def legendre_table(band_count):
    centre = (2.0 * jnp.arange(band_count, dtype=jnp.float32) + 1.0) / band_count - 1.0
    return jnp.stack(
        [
            jnp.ones_like(centre),
            centre,
            0.5 * (3.0 * centre * centre - 1.0),
            0.5 * (5.0 * centre * centre * centre - 3.0 * centre),
        ],
        axis=1,
    )


def gram_solve(gram_matrix, rhs_rows):
    chol_lower = jnp.linalg.cholesky(gram_matrix)
    forward = []
    for row_at in range(4):
        current = rhs_rows[row_at]
        for col_at in range(row_at):
            current = current - chol_lower[row_at, col_at] * forward[col_at]
        forward.append(current / chol_lower[row_at, row_at])
    backward = [forward[0]] * 4
    for row_at in (3, 2, 1, 0):
        current = forward[row_at]
        for col_at in range(row_at + 1, 4):
            current = current - chol_lower[col_at, row_at] * backward[col_at]
        backward[row_at] = current / chol_lower[row_at, row_at]
    return jnp.stack(backward)


def coherence(direction, own_table, all_table, weights, block_span):
    offset = direction * block_span
    own_real = lax.dynamic_slice_in_dim(own_table[0], offset, block_span, 1)
    own_imag = lax.dynamic_slice_in_dim(own_table[1], offset, block_span, 1)
    weight_block = lax.dynamic_slice_in_dim(weights, offset, block_span, 1)
    blocks = []
    for flux_at in range(3):
        factor_row = weight_block[flux_at][None, :]
        blocks.append(
            jnp.concatenate([own_real * factor_row, own_imag * factor_row], 1).astype(jnp.bfloat16)
        )
    operand_left = jnp.concatenate(blocks, 0)
    far_real = lax.dynamic_slice_in_dim(all_table[0], offset, block_span, 1)
    far_imag = lax.dynamic_slice_in_dim(all_table[1], offset, block_span, 1)
    operand_right = jnp.concatenate(
        [jnp.concatenate([far_real, far_imag], 1), jnp.concatenate([-far_imag, far_real], 1)], 0
    )
    product = lax.dot_general(
        operand_left, operand_right, (((1,), (1,)), ((), ())), preferred_element_type=jnp.float32
    )
    row_count = own_real.shape[0]
    col_count = far_real.shape[0]
    entries = [
        (
            product[flux_at * row_count : (flux_at + 1) * row_count, :col_count],
            product[flux_at * row_count : (flux_at + 1) * row_count, col_count:],
        )
        for flux_at in range(3)
    ]
    return [entries[0], entries[1], entries[1], entries[2]]


def residual_of(
    band_vis, mask_float, near_gains, far_gains, own_table, all_table, weights, block_span
):

    def residual_direction_step(model_sum, direction):
        coh_matrix = coherence(direction, own_table, all_table, weights, block_span)
        near_jones = unpack_matrix(
            lax.dynamic_index_in_dim(near_gains, direction, 1, keepdims=False)[:, :, None]
        )
        far_jones = unpack_matrix(
            lax.dynamic_index_in_dim(far_gains, direction, 1, keepdims=False)[:, None, :]
        )
        model_term = matrix_mul(matrix_mul(near_jones, coh_matrix), matrix_herm(far_jones))
        return (model_sum + pack_matrix(model_term), None)

    model_sum, _ = lax.scan(
        residual_direction_step,
        jnp.zeros(band_vis.shape, jnp.float32),
        jnp.arange(near_gains.shape[1], dtype=jnp.int32),
    )
    return (band_vis - model_sum) * mask_float[None]


def gradient_of(residual, near_gains, far_gains, own_table, all_table, weights, block_span):
    res_matrix = unpack_matrix(residual)

    def gradient_direction_step(state_value, direction):
        coh_matrix = coherence(direction, own_table, all_table, weights, block_span)
        near_jones = unpack_matrix(
            lax.dynamic_index_in_dim(near_gains, direction, 1, keepdims=False)[:, :, None]
        )
        far_jones = unpack_matrix(
            lax.dynamic_index_in_dim(far_gains, direction, 1, keepdims=False)[:, None, :]
        )
        col_part = matrix_mul(matrix_herm(res_matrix), matrix_mul(near_jones, coh_matrix))
        row_part = matrix_mul(res_matrix, matrix_mul(far_jones, matrix_herm(coh_matrix)))
        return (state_value, (summed_pack(row_part, 1), summed_pack(col_part, 0)))

    _, (row_terms, col_terms) = lax.scan(
        gradient_direction_step,
        jnp.zeros((), jnp.float32),
        jnp.arange(near_gains.shape[1], dtype=jnp.int32),
    )
    return (row_terms, col_terms)


def local(
    visibilities,
    flag_mask,
    stations,
    directions,
    intensity,
    polarized,
    spectral,
    clusters,
    jones_gains,
    scaled_duals,
    consensus,
):
    band_count = lax.axis_size("freq")
    band_index = lax.axis_index("freq")
    block_count = lax.axis_size("stn")
    sort_order = jnp.argsort(clusters, stable=True)
    sky_dirs = directions[:, sort_order]
    sky_flux = intensity[sort_order]
    sky_pol = polarized[:, sort_order]
    sky_index = spectral[sort_order]
    block_span = clusters.shape[0] // DIRS
    freq_ratio = band_ratio(band_index, band_count)
    weights = flux_weights(sky_flux, sky_pol, sky_index, freq_ratio)
    own_gains = jones_gains[0]
    own_duals = scaled_duals[0]
    station_rows = own_gains.shape[2]
    own_table = station_table(stations, sky_dirs, freq_ratio)
    all_table = lax.all_gather(own_table, "stn", axis=1, tiled=True)
    all_gains = lax.all_gather(own_gains, "stn", axis=2, tiled=True)
    residual = residual_of(
        visibilities[0],
        flag_mask.astype(jnp.float32),
        own_gains,
        all_gains,
        own_table,
        all_table,
        weights,
        block_span,
    )
    row_terms, col_terms = gradient_of(
        residual, own_gains, all_gains, own_table, all_table, weights, block_span
    )
    basis_table = legendre_table(band_count)
    basis_row = lax.dynamic_index_in_dim(basis_table, band_index, 0, keepdims=False)
    poly_value = jnp.sum(basis_row[:, None, None, None] * consensus, 0)
    penalty_term = PENALTY / 2.0 * (own_gains - poly_value + own_duals)
    own_columns = lax.psum_scatter(col_terms, "stn", scatter_dimension=2, tiled=True)
    drive = jnp.transpose(row_terms + own_columns, (1, 0, 2)) + penalty_term
    total_sq = lax.psum(jnp.sum(drive * drive), "stn")
    entry_count = drive.shape[0] * drive.shape[1] * station_rows * block_count
    step_length = STEP_SIZE / jnp.sqrt(total_sq / entry_count + 1e-06)
    jones_next = own_gains - step_length * drive
    weighted_sum = basis_row[:, None, None, None] * (jones_next + own_duals)[None]
    summed = lax.psum(weighted_sum, "freq")
    gram_matrix = jnp.dot(basis_table.T, basis_table, precision=lax.Precision.HIGHEST)
    consensus_next = gram_solve(gram_matrix, summed.reshape(4, -1)).reshape(summed.shape)
    poly_next = jnp.sum(basis_row[:, None, None, None] * consensus_next, 0)
    duals_next = own_duals + jones_next - poly_next
    return (jones_next[None], duals_next[None], consensus_next)


def solution(mesh):
    placed = (
        P("freq", None, "stn", None),
        P("stn", None),
        P(None, "stn"),
        P(),
        P(),
        P(),
        P(),
        P(),
        P("freq", None, None, "stn"),
        P("freq", None, None, "stn"),
        P(None, None, None, "stn"),
    )
    return jax.shard_map(
        local,
        mesh=mesh,
        in_specs=placed,
        out_specs=(
            P("freq", None, None, "stn"),
            P("freq", None, None, "stn"),
            P(None, None, None, "stn"),
        ),
        check_vma=False,
    )
```

profile of v0, /device:TPU:1, one launch (start us, length us, event | category | flops | bytes accessed | tf_op | source)
XLA Modules:
  0.0 979.8 jit_solution(6484654499400362733)
XLA Ops:
  9.0 5.7 sort.17
  14.8 2.6 gather_fusion
  21.3 57.3 %all-gather = f32[1,8,16,1024]{2,1,0,3:T(8,128)} all-gather(f32[1,8,16,64]{2,1,0,3:T(8,128)S(1)} %copy.65), channel_id=2, replica_groups=mesh['freq'=16,'stn'=16] {'stn'}, dimensions={3}, use_global_device_ids=true | all-gather | bytes 557056 | tf_op jit(solution)/shard_map/all_gather | solution.py:237
  78.6 3.7 copy.71
  82.3 8.4 gather_fusion.1
  90.7 8.4 gather_fusion.3
  99.4 2.6 gather_fusion.2
  104.2 335.2 %while.25 = (s32[]{:T(128)}, f32[8,64,1024]{2,1,0:T(8,128)}, s32[16]{0:T(128)}, f32[8,16,64]{2,1,0:T(8,128)}, bf16[2,64,1536]{2,1,0:T(8,128)(2,1)S(1)}, /*index=...) while((s32[]{:T(128)}, f32[8,64,1024]{2,1,0:T(8,128)}, ...), condition=%wide.region_2.3_spmd.clone, body=%wide.region_1.2_spmd.clone.sunk | while | flops 163356688 | bytes 62084416 | solution.py:177
  108.6 4.9 fusion.126
  129.6 4.9 fusion.126
  150.5 4.9 fusion.126
  171.5 4.9 fusion.126
  192.5 4.9 fusion.126
  213.4 4.9 fusion.126
  234.4 4.9 fusion.126
  255.3 4.9 fusion.126
  276.3 4.9 fusion.126
  297.2 4.9 fusion.126
  318.2 4.9 fusion.126
  339.2 4.9 fusion.126
  360.1 4.9 fusion.126
  381.1 4.9 fusion.126
  402.0 4.9 fusion.126
  423.0 4.9 fusion.126
  439.4 2.7 fusion.72
  444.5 334.4 %while.24 = (s32[]{:T(128)}, f32[16,8,64]{2,0,1:T(8,128)}, f32[16,8,1024]{2,1,0:T(8,128)}, s32[16]{0:T(128)S(1)}, f32[8,16,1024]{2,1,0:T(8,128)}, /*index=5*/bf1...) while((s32[]{:T(128)}, f32[16,8,64]{2,0,1:T(8,128)}, ...), condition=%wide.region_20.21_spmd, body=%wide.region_3.20_spmd.sunk | while | flops 171216896 | bytes 51090484 | solution.py:200
  444.5 4.9 fusion.118
  465.4 5.0 fusion.118
  486.3 5.0 fusion.118
  507.2 5.0 fusion.118
  528.1 5.0 fusion.118
  549.0 5.0 fusion.118
  569.9 5.0 fusion.118
  590.8 5.0 fusion.118
  611.7 5.0 fusion.118
  632.6 5.0 fusion.118
  653.5 5.0 fusion.118
  674.4 5.0 fusion.118
  695.3 5.0 fusion.118
  716.2 5.0 fusion.118
  737.1 5.0 fusion.118
  758.0 5.0 fusion.118
  778.8 3.6 copy.75
  782.5 4.0 reshape.829
  788.2 50.0 %reduce-scatter.4.cloned.1.call-done = f32[64,128]{1,0:T(8,128)} async-done(((f32[1024,128]{1,0:T(8,128)}), f32[64,128]{1,0:T(8,128)}) %reduce-scatter.4.cloned.1.call-update) | async-done | bytes 32784
  840.7 27.0 %psum.14 = f32[]{:T(128)} all-reduce(f32[]{:T(128)} %get-tuple-element.504), channel_id=1, replica_groups=mesh['freq'=16,'stn'=16] {'stn'}, use_global_device_ids=true, to_apply=%region_24.25 | all-reduce | flops 1 | bytes 8 | tf_op jit(solution)/shard_map/psum | solution.py:257
  873.4 91.9 %all-reduce.2.cloned.1.call-done = f32[4,8,16,64]{3,2,1,0:T(8,128)} async-done(((f32[4,8,16,64]{3,2,1,0:T(8,128)}), f32[4,8,16,64]{3,2,1,0:T(8,128)}) %all-reduce.2.cloned.1.call-update) | async-done | bytes 131088 | tf_op jit(solution)/shard_map/psum | solution.py:262
  965.2 6.6 subtract_divide_fusion
  (1475 shorter events, 445.5 us)
Async XLA Ops:
  7.2 75.1 %copy-start = (f32[1536]{0:T(1024)S(1)}, f32[1536]{0:T(1024)}, u32[]{:S(2)}) copy-start(f32[1536]{0:T(1024)} %param.19) | copy-start | bytes 18436
  7.2 96.5 %all-gather.3.cloned.1.call-start = ((), (), s32[]{:S(2)}) async-start(), calls=%async_computation.1 | async-start | bytes 6684672 | tf_op jit(solution)/shard_map/all_gather | solution.py:236
  20.2 818.0 %reduce-scatter.4.cloned.1.call-start = ((), (), s32[]{:S(2)}) async-start(), calls=%async_computation.3 | async-start | bytes 557056
  82.3 8.4 copy-start.1
  90.7 8.4 copy-start.28
  90.7 11.6 %copy-start.25 = (s32[64,1024]{1,0:T(8,128)S(1)}, s32[64,1024]{1,0:T(8,128)}, u32[]{:S(2)}) copy-start(s32[64,1024]{1,0:T(8,128)} %param.16) | copy-start | bytes 786436
  99.1 5.1 copy-start.5
  116.4 1.5 copy-start.18
  119.2 2.3 copy-start.2
  140.2 2.3 copy-start.2
  161.1 2.3 copy-start.2
  179.3 1.5 copy-start.18
  182.1 2.3 copy-start.2
  203.0 2.3 copy-start.2
  221.2 1.5 copy-start.18
  224.0 2.3 copy-start.2
  245.0 2.3 copy-start.2
  265.9 2.3 copy-start.2
  286.9 2.3 copy-start.2
  307.8 2.3 copy-start.2
  326.0 1.5 copy-start.18
  328.8 2.3 copy-start.2
  349.7 2.3 copy-start.2
  370.7 2.3 copy-start.2
  388.9 1.5 copy-start.18
  391.7 2.3 copy-start.2
  412.6 2.3 copy-start.2
  433.5 2.3 copy-start.2
  444.5 5.0 copy-start.29
  465.4 5.0 copy-start.29
  486.3 5.0 copy-start.29
  507.2 5.0 copy-start.29
  528.1 5.0 copy-start.29
  549.0 5.0 copy-start.29
  569.9 5.0 copy-start.29
  590.8 5.0 copy-start.29
  611.7 5.0 copy-start.29
  632.6 5.0 copy-start.29
  653.5 5.0 copy-start.29
  674.4 5.0 copy-start.29
  695.3 5.0 copy-start.29
  716.2 5.0 copy-start.29
  737.1 5.0 copy-start.29
  758.0 5.0 copy-start.29
  782.5 5.7 copy-start.24
  782.5 56.8 %copy-start.26 = (f32[1,8,16,64]{3,2,1,0:T(8,128)S(1)}, f32[1,8,16,64]{3,2,1,0:T(8,128)}, u32[]{:S(2)}) copy-start(f32[1,8,16,64]{3,2,1,0:T(8,128)} %param.24) | copy-start | bytes 98308
  782.5 56.8 %copy-start.27 = (f32[16,8,64]{2,0,1:T(8,128)S(1)}, f32[16,8,64]{2,0,1:T(8,128)}, u32[]{:S(2)}) copy-start(f32[16,8,64]{2,0,1:T(8,128)} %get-tuple-element.221) | copy-start | bytes 98308
  786.5 178.8 %all-reduce.2.cloned.1.call-start = ((), (), s32[]{:S(2)}) async-start(), calls=%async_computation.2 | async-start | bytes 524288 | tf_op jit(solution)/shard_map/psum | solution.py:262
  (331 other events, 367.8 us)
Sparse Core Ops, SparseCore 0:
  20.3 66.2 all-gather.2
  786.6 51.5 reduce-scatter.3
  870.9 94.3 all-reduce.1
where the time goes:
time: 992 us; the launch traced here: 980 us
  local copies, waits for them, and re-layouts  416 us (42%)
  other arithmetic  216 us (22%)
  waiting for transfers between devices  142 us (14%)
  loops' own time  85.4 us (9%)
  blocking collectives  84.4 us (9%)
  matrix products  20.2 us (2%)
  between operations  16 us (2%)
    slice x32, local copies, waits for them, and re-layouts, coherence(): far_imag = lax.dynamic_slice_in_dim(all_table[1], offset, block_span, 1)  158 us
    psum x1, waiting for transfers between devices, local(): summed = lax.psum(weighted_sum, 'freq')  91.9 us
    while x736, local copies, waits for them, and re-layouts  81.8 us
    all_gather x1, blocking collectives, local(): all_gains = lax.all_gather(own_gains, 'stn', axis=2, tiled=True)  57.3 us
    unnamed x4, waiting for transfers between devices  50 us
    another operation x1, loops' own time, gradient_of(): lax.scan(gradient_direction_step, jnp.zeros((), jnp.float32), jnp.arange(...  46.3 us
    another operation x1, loops' own time, residual_of(): lax.scan(residual_direction_step, jnp.zeros(band_vis.shape, jnp.float32),...  39.1 us
    neg x32, other arithmetic, coherence(): -far_imag  37.9 us
  transfers between devices with their start and end apart: 3, of which 2 were waited for; matrix products, arithmetic and copies ran while one was open for 3% of the time, Pallas kernels for 0%

commit v1 on v0

v1 whole, which is shorter than its diff:
```python
import math

import jax
import jax.numpy as jnp
import numpy as np
from jax import lax
from jax.experimental import pallas as pl
from jax.experimental.pallas import tpu as pltpu
from jax.sharding import PartitionSpec as P

DIRS = 16
COMPS = 1536
BANDS = 16
BLOCKS = 16
NS = 1024
OWN = 64
ENTRIES = 131072
PENALTY = 40.0
STEP_SIZE = 0.5
F32 = jnp.float32
BF16 = jnp.bfloat16
SPAN = 128
STEPS = COMPS // SPAN
VMEM = pl.BlockSpec(memory_space=pltpu.VMEM)
SMEM = pl.BlockSpec(memory_space=pltpu.SMEM)


def turn_polynomials():
    nodes = (np.cos(np.pi * (np.arange(64) + 0.5) / 64) + 1.0) / 8.0
    root = np.sqrt(nodes)
    cos_fit = np.polynomial.Chebyshev.fit(nodes, np.cos(2 * np.pi * root), 6, domain=[0, 0.25])
    sin_fit = np.polynomial.Chebyshev.fit(
        nodes, -np.sin(2 * np.pi * root) / root, 5, domain=[0, 0.25]
    )
    to_list = lambda fit: [float(v) for v in fit.convert(kind=np.polynomial.Polynomial).coef]
    return to_list(cos_fit), to_list(sin_fit)


COS_POLY, SIN_POLY = turn_polynomials()


def legendre_rows():
    centre = (2.0 * np.arange(BANDS) + 1.0) / BANDS - 1.0
    return np.stack(
        [
            np.ones_like(centre),
            centre,
            0.5 * (3.0 * centre * centre - 1.0),
            0.5 * (5.0 * centre * centre * centre - 3.0 * centre),
        ],
        axis=1,
    )


def horner(coefs, value):
    total = coefs[-1]
    for coef in coefs[-2::-1]:
        total = total * value + coef
    return total


def phases(turns):
    frac = turns - jnp.floor(turns + 0.5)
    square = frac * frac
    real = horner(COS_POLY, square)
    imag = frac * horner(SIN_POLY, square)
    return real.astype(BF16).astype(F32), imag.astype(BF16).astype(F32)


def split3(value):
    high = value.astype(BF16).astype(F32)
    rest = value - high
    middle = rest.astype(BF16).astype(F32)
    return high, middle, (rest - middle).astype(BF16).astype(F32)


def band_basis(band):
    centre = (2.0 * band.astype(F32) + 1.0) / BANDS - 1.0
    return (
        jnp.float32(1.0),
        centre,
        0.5 * (3.0 * centre * centre - 1.0),
        0.5 * (5.0 * centre * centre * centre - 3.0 * centre),
    )


def gains_rows(ref, lead=()):
    groups = []
    for column in range(2):
        for part in range(2):
            at = 2 * column + part
            groups.append(jnp.concatenate([ref[lead + (at,)], ref[lead + (4 + at,)]], axis=1))
    return jnp.concatenate(groups, axis=0)


def put_gains(ref, rows, lead=()):
    for column in range(2):
        for part in range(2):
            at = 2 * column + part
            group = rows[at * 16 : at * 16 + 16]
            ref[lead + (at,)] = group[:, :64]
            ref[lead + (4 + at,)] = group[:, 64:]


def packet_kernel(jones_ref, stations_ref, own_ref, copies_ref):
    place = jnp.concatenate([stations_ref[...], stations_ref[...]], axis=1)
    rows = jnp.concatenate([gains_rows(jones_ref), place, jnp.zeros((5, 128), F32)], axis=0)
    own_ref[...] = rows
    copies_ref[...] = jnp.broadcast_to(rows[None], copies_ref.shape)


def prepare_kernel(
    band_ref,
    vis_ref,
    mask_ref,
    dirs_ref,
    flux_ref,
    pol_ref,
    index_ref,
    clusters_ref,
    out_ref,
    sky_ref,
):
    @pl.when(pl.program_id(0) == 0)
    def _():
        prepare_sky(band_ref, dirs_ref, flux_ref, pol_ref, index_ref, clusters_ref, sky_ref)

    mask = mask_ref[...].astype(F32)

    def put(pair, real, imag):
        turned = jnp.concatenate([real, imag], axis=0).T.astype(BF16)
        for dest in range(2):
            out_ref[dest, pair * 64 : pair * 64 + 64, :] = turned[dest * 64 : dest * 64 + 64]

    for pair in range(4):
        put(pair, vis_ref[2 * pair] * mask, vis_ref[2 * pair + 1] * mask)
    put(4, mask, mask)


def flat(ref):
    return jnp.concatenate([ref[at : at + 1, :] for at in range(COMPS // 128)], axis=1)


def prepare_sky(band_ref, dirs_ref, flux_ref, pol_ref, index_ref, clusters_ref, out_ref):
    ratio = 0.5 + 3.0 * (band_ref[0].astype(F32) + 0.5) / BANDS
    dir_l = dirs_ref[0:1, :]
    dir_m = dirs_ref[1:2, :]
    dir_n = jnp.sqrt(1.0 - dir_l * dir_l - dir_m * dir_m) - 1.0
    log_ratio = jnp.log(jnp.full((1, COMPS), ratio, F32))
    factor = jnp.exp(flat(index_ref) * log_ratio)
    flux = flat(flux_ref)
    stokes_q = pol_ref[0:1, :]
    rows = [
        dir_l * ratio,
        dir_m * ratio,
        dir_n * ratio,
        (flux + stokes_q) * factor,
        pol_ref[1:2, :] * factor,
        (flux - stokes_q) * factor,
    ]
    row_at = lax.broadcasted_iota(jnp.int32, (8, COMPS), 0)
    stacked = jnp.zeros((8, COMPS), F32)
    for at, row in enumerate(rows):
        stacked = jnp.where(row_at == at, row, stacked)
    high, middle, low = split3(stacked)
    table = jnp.concatenate(
        [high, high, high, middle, middle, low, jnp.zeros((80, COMPS), F32)], axis=0
    ).astype(BF16)
    clusters = flat(clusters_ref)
    hot = (lax.broadcasted_iota(jnp.int32, (16, COMPS), 0) == clusters).astype(F32)
    before = (
        lax.broadcasted_iota(jnp.int32, (128, 128), 0)
        < lax.broadcasted_iota(jnp.int32, (128, 128), 1)
    ).astype(BF16)
    seen = jnp.zeros((16, 1), F32)
    ranks = []
    for at in range(COMPS // 128):
        part = hot[:, at * 128 : at * 128 + 128]
        inside = jnp.dot(part.astype(BF16), before, preferred_element_type=F32) + seen
        ranks.append(jnp.sum(inside * part, axis=0, keepdims=True))
        seen = seen + jnp.sum(part, axis=1, keepdims=True)
    place = 16 * jnp.concatenate(ranks, axis=1).astype(jnp.int32) + clusters
    for at in range(COMPS // 256):
        target = lax.broadcasted_iota(jnp.int32, (256, COMPS), 0) + at * 256
        chosen = (target == place).astype(F32).astype(BF16)
        out_ref[at * 256 : at * 256 + 256, :] = lax.dot_general(
            chosen, table, (((1,), (1,)), ((), ())), preferred_element_type=F32
        ).astype(BF16)


def station_operand(rows8):
    high, middle, low = split3(rows8)
    width = rows8.shape[1]
    return jnp.concatenate(
        [high, middle, low, high, middle, high, jnp.zeros((80, width), F32)], axis=0
    ).astype(BF16)


def model_kernel(
    sky_ref, all_ref, own_ref, far_ref, weighted_ref, model_ref, geo_ref, geo_own_ref, gains_ref, turns_ref
):
    step = pl.program_id(0)
    lower = lax.broadcasted_iota(jnp.int32, (1, 128), 1) < 64

    @pl.when(step == 0)
    def _():
        model_ref[...] = jnp.zeros_like(model_ref)
        geo_own_ref[...] = station_operand(own_ref[64:72, :])
        for tile in range(8):
            first, second = all_ref[2 * tile], all_ref[2 * tile + 1]
            lanes = slice(tile * 128, tile * 128 + 128)
            geo_ref[:, lanes] = station_operand(jnp.where(lower, first[64:72], second[64:72]))
            low_part = jnp.where(lower, first[0:64], pltpu.roll(second[0:64], 64, 1))
            high_part = jnp.where(lower, pltpu.roll(first[0:64], 64, 1), second[0:64])
            gains_ref[:, lanes] = low_part
            gains_ref[:, 1024 + tile * 128 : 1024 + tile * 128 + 128] = high_part

    sky = sky_ref[...]
    turns_ref[...] = jnp.dot(sky, geo_ref[...], preferred_element_type=F32)

    def rows_step(at, carry):
        rows = pl.ds(pl.multiple_of(at * 16, 16), 16)
        for lane in range(0, NS, 256):
            real, imag = phases(turns_ref[rows, lane : lane + 256])
            for row in range(2):
                lanes = slice(row * NS + lane, row * NS + lane + 256)
                for column in range(2):
                    gain_re = gains_ref[column * 32 : column * 32 + 16, lanes]
                    gain_im = gains_ref[column * 32 + 16 : column * 32 + 32, lanes]
                    far_ref[column, rows, lanes] = (real * gain_re - imag * gain_im).astype(BF16)
                    far_ref[2 + column, rows, lanes] = (real * gain_im + imag * gain_re).astype(
                        BF16
                    )
        return carry

    lax.fori_loop(0, SPAN // 16, rows_step, 0)

    own_re, own_im = phases(jnp.dot(sky, geo_own_ref[...], preferred_element_type=F32))
    source = lax.broadcasted_iota(jnp.int32, (128, 384), 0)
    target = 3 + lax.broadcasted_iota(jnp.int32, (128, 384), 1) // 128
    select = (source == target) | (source == target + 24) | (source == target + 40)
    weights = jnp.dot(sky, select.astype(F32).astype(BF16), preferred_element_type=F32)
    weighted = []
    for flux in range(3):
        weight = weights[:, flux * 128 : flux * 128 + 128]
        pair = ((own_re * weight).astype(BF16), (own_im * weight).astype(BF16))
        weighted_ref[2 * flux] = pair[0]
        weighted_ref[2 * flux + 1] = pair[1]
        weighted.append((pair[0].astype(F32), pair[1].astype(F32)))
    gains = [jnp.concatenate([own_ref[at * 16 : at * 16 + 16]] * 8, axis=0) for at in range(4)]
    near_re, near_im = [], []
    for first, second in ((0, 1), (1, 2)):
        (ar, ai), (br, bi) = weighted[first], weighted[second]
        real = gains[0] * ar - gains[1] * ai + gains[2] * br - gains[3] * bi
        imag = gains[0] * ai + gains[1] * ar + gains[2] * bi + gains[3] * br
        near_re.append(real.T)
        near_im.append(imag.T)
    near = jnp.concatenate(
        [
            jnp.concatenate(near_re + near_im, axis=1),
            jnp.concatenate(near_im + [-near_re[0], -near_re[1]], axis=1),
        ],
        axis=0,
    ).astype(BF16)
    far = far_ref[...].reshape(4 * SPAN, 2 * NS)
    model_ref[...] += jnp.dot(near, far, preferred_element_type=F32)


def gradient_kernel(
    band_ref,
    block_ref,
    far_ref,
    weighted_ref,
    vis_ref,
    mask_ref,
    got_ref,
    model_ref,
    own_ref,
    duals_ref,
    consensus_ref,
    drive_ref,
    square_ref,
    both_ref,
    near_ref,
    sum_ref,
):
    step = pl.program_id(0)
    own_tile = block_ref[0] // 2

    @pl.when(step == 0)
    def _():
        sum_ref[...] = jnp.zeros_like(sum_ref)
        lower = lax.broadcasted_iota(jnp.int32, (1, 128), 1) < 64
        for tile in range(8):
            lanes = slice(tile * 128, tile * 128 + 128)
            mask = mask_ref[:, lanes].astype(F32)

            def halves(pair):
                first = got_ref[2 * tile, pair * 64 : pair * 64 + 64, :].astype(F32)
                second = got_ref[2 * tile + 1, pair * 64 : pair * 64 + 64, :].astype(F32)
                return first, second

            first, second = halves(4)
            mask_both = mask + jnp.where(lower, first, second)
            for row in range(2):
                for column in range(2):
                    first, second = halves(2 * column + row)
                    real = jnp.where(lower, first, pltpu.roll(second, 64, 1))
                    imag = jnp.where(lower, pltpu.roll(first, 64, 1), second)
                    at = column * NS + tile * 128
                    for part, other in ((0, real), (1, -imag)):
                        top = part * 128 + row * 64
                        vis = vis_ref[4 * row + 2 * column + part, :, lanes]
                        model = model_ref[top : top + 64, at : at + 128]
                        value = vis * mask + other - mask_both * model
                        high = value.astype(BF16)
                        both_ref[top : top + 64, at : at + 128] = high

                        @pl.when(tile == own_tile)
                        def _(value=value, high=high, top=top, column=column):
                            near_ref[top : top + 64, column * 128 : column * 128 + 128] = (
                                value - high.astype(F32)
                            ).astype(BF16)

    product = lax.dot_general(
        far_ref[...].reshape(4 * SPAN, 2 * NS),
        both_ref[...],
        (((1,), (1,)), ((), ())),
        preferred_element_type=F32,
    )
    lane = pl.multiple_of(own_tile * 128, 128)
    beside = jnp.concatenate(
        [
            far_ref[:, :, pl.ds(lane, 128)].reshape(4 * SPAN, 128),
            far_ref[:, :, pl.ds(NS + lane, 128)].reshape(4 * SPAN, 128),
        ],
        axis=1,
    )
    product = product + lax.dot_general(
        beside, near_ref[...], (((1,), (1,)), ((), ())), preferred_element_type=F32
    )
    terms = []
    for column in range(2):
        real_rows = product[column * SPAN : column * SPAN + SPAN]
        imag_rows = product[(2 + column) * SPAN : (2 + column) * SPAN + SPAN]
        terms.append(
            (
                real_rows[:, :128] - imag_rows[:, 128:],
                imag_rows[:, :128] + real_rows[:, 128:],
            )
        )
    weighted = [weighted_ref[at].astype(F32) for at in range(6)]
    for column, (first, second) in enumerate(((0, 1), (1, 2))):
        real = jnp.zeros((SPAN, 128), F32)
        imag = jnp.zeros((SPAN, 128), F32)
        for (tr, ti), flux in zip(terms, (first, second)):
            wr, wi = weighted[2 * flux], weighted[2 * flux + 1]
            real = real + (tr * wr + ti * wi)
            imag = imag + (ti * wr - tr * wi)
        for part, value in enumerate((real, imag)):
            at = (2 * column + part) * 16
            sum_ref[at : at + 16] += jnp.sum(value.reshape(SPAN // 16, 16, 128), axis=0)

    @pl.when(step == STEPS - 1)
    def _():
        basis = band_basis(band_ref[0])
        poly = jnp.zeros((64, 128), F32)
        for at in range(4):
            poly = poly + basis[at] * gains_rows(consensus_ref, (at,))
        penalty = PENALTY / 2.0 * (own_ref[0:64, :] - poly + gains_rows(duals_ref))
        drive = penalty - sum_ref[...]
        drive_ref[...] = drive
        square_ref[...] = jnp.broadcast_to(
            jnp.sum(drive * drive, axis=0, keepdims=True), square_ref.shape
        )


def update_kernel(squares_ref, drive_ref, own_ref, duals_ref, next_ref, shared_ref):
    total = jnp.sum(squares_ref[...], axis=(0, 1), keepdims=True)
    length = STEP_SIZE / jnp.sqrt(total / ENTRIES + 1e-6)
    rows = own_ref[0:64, :] - length * drive_ref[...]
    put_gains(next_ref, rows)
    shared_ref[...] = jnp.broadcast_to((rows + gains_rows(duals_ref))[None], shared_ref.shape)


def finish_kernel(band_ref, shared_ref, own_ref, duals_ref, consensus_ref):
    table = legendre_rows()
    gram = table.T @ table
    lower = np.linalg.cholesky(gram)
    sums = []
    for at in range(4):
        total = shared_ref[0] * float(table[0, at])
        for band in range(1, BANDS):
            total = total + shared_ref[band] * float(table[band, at])
        sums.append(total)
    forward = []
    for row in range(4):
        current = sums[row]
        for col in range(row):
            current = current - float(lower[row, col]) * forward[col]
        forward.append(current * float(1.0 / lower[row, row]))
    backward = [None] * 4
    for row in (3, 2, 1, 0):
        current = forward[row]
        for col in range(row + 1, 4):
            current = current - float(lower[col, row]) * backward[col]
        backward[row] = current * float(1.0 / lower[row, row])
    basis = band_basis(band_ref[0])
    poly = jnp.zeros((64, 128), F32)
    for at in range(4):
        put_gains(consensus_ref, backward[at], (at,))
        poly = poly + basis[at] * backward[at]
    put_gains(duals_ref, own_ref[0] - poly)


def cost(flops, moved):
    return pl.CostEstimate(flops=int(flops), bytes_accessed=int(moved), transcendentals=0)


def local(
    visibilities,
    flag_mask,
    stations,
    directions,
    intensity,
    polarized,
    spectral,
    clusters,
    jones_gains,
    scaled_duals,
    consensus,
):
    band = lax.axis_index("freq").reshape(1).astype(jnp.int32)
    block = lax.axis_index("stn").reshape(1).astype(jnp.int32)
    vis, jones, duals = visibilities[0], jones_gains[0], scaled_duals[0]
    shape = jax.ShapeDtypeStruct
    big = pltpu.CompilerParams(vmem_limit_bytes=56 * 1024 * 1024)
    own, copies = pl.pallas_call(
        packet_kernel,
        out_shape=[shape((72, 128), F32), shape((BLOCKS, 72, 128), F32)],
        in_specs=[VMEM] * 2,
        out_specs=[VMEM, VMEM],
        name="packet",
    )(jones, stations)
    everyone = lax.all_to_all(copies, "stn", 0, 0, tiled=True)
    outgoing, sky = pl.pallas_call(
        prepare_kernel,
        grid=(8,),
        in_specs=[
            SMEM,
            pl.BlockSpec((8, OWN, 128), lambda at: (0, 0, at)),
            pl.BlockSpec((OWN, 128), lambda at: (0, at)),
        ]
        + [VMEM] * 5,
        out_specs=[pl.BlockSpec((2, 320, 128), lambda at: (at, 0, 0)), VMEM],
        out_shape=[shape((BLOCKS, 320, 128), BF16), shape((COMPS, 128), BF16)],
        compiler_params=big,
        cost_estimate=cost(4e9, 1e6),
        name="prepare",
    )(
        band,
        vis,
        flag_mask,
        directions,
        intensity.reshape(COMPS // 128, 128),
        polarized,
        spectral.reshape(COMPS // 128, 128),
        clusters.reshape(COMPS // 128, 128),
    )
    incoming = lax.all_to_all(outgoing, "stn", 0, 0, tiled=True)
    far, weighted, model = pl.pallas_call(
        model_kernel,
        grid=(STEPS,),
        in_specs=[
            pl.BlockSpec((SPAN, 128), lambda at: (at, 0)),
            VMEM,
            VMEM,
        ],
        out_specs=[
            pl.BlockSpec((4, SPAN, 2 * NS), lambda at: (0, at, 0)),
            pl.BlockSpec((6, SPAN, 128), lambda at: (0, at, 0)),
            pl.BlockSpec((256, 2 * NS), lambda at: (0, 0)),
        ],
        out_shape=[
            shape((4, COMPS, 2 * NS), BF16),
            shape((6, COMPS, 128), BF16),
            shape((256, 2 * NS), F32),
        ],
        scratch_shapes=[
            pltpu.VMEM((128, NS), BF16),
            pltpu.VMEM((128, 128), BF16),
            pltpu.VMEM((64, 2 * NS), F32),
            pltpu.VMEM((SPAN, NS), F32),
        ],
        compiler_params=big,
        cost_estimate=cost(2e10, 4e7),
        name="model",
    )(sky, everyone, own)
    drive, squares = pl.pallas_call(
        gradient_kernel,
        grid=(STEPS,),
        in_specs=[
            SMEM,
            SMEM,
            pl.BlockSpec((4, SPAN, 2 * NS), lambda at: (0, at, 0)),
            pl.BlockSpec((6, SPAN, 128), lambda at: (0, at, 0)),
        ]
        + [VMEM] * 7,
        out_specs=[VMEM, VMEM],
        out_shape=[shape((64, 128), F32), shape((BLOCKS, 128), F32)],
        scratch_shapes=[
            pltpu.VMEM((256, 2 * NS), BF16),
            pltpu.VMEM((256, 256), BF16),
            pltpu.VMEM((64, 128), F32),
        ],
        compiler_params=big,
        cost_estimate=cost(7e9, 3e7),
        name="gradient",
    )(band, block, far, weighted, vis, flag_mask, incoming, model, own, duals, consensus)
    squares = lax.all_to_all(squares, "stn", 0, 0, tiled=True)
    jones_next, shared = pl.pallas_call(
        update_kernel,
        out_shape=[shape((8, DIRS, OWN), F32), shape((BANDS, 64, 128), F32)],
        in_specs=[VMEM] * 4,
        out_specs=[VMEM, VMEM],
        name="update",
    )(squares, drive, own, duals)
    gathered = lax.all_to_all(shared, "freq", 0, 0, tiled=True)
    duals_next, consensus_next = pl.pallas_call(
        finish_kernel,
        grid=(1,),
        out_shape=[shape((8, DIRS, OWN), F32), shape((4, 8, DIRS, OWN), F32)],
        in_specs=[SMEM, VMEM, pl.BlockSpec((1, 64, 128), lambda at: (0, 0, 0))],
        out_specs=[VMEM, VMEM],
        name="finish",
    )(band, gathered, shared)
    return (jones_next[None], duals_next[None], consensus_next)


def solution(mesh):
    placed = (
        P("freq", None, "stn", None),
        P("stn", None),
        P(None, "stn"),
        P(),
        P(),
        P(),
        P(),
        P(),
        P("freq", None, None, "stn"),
        P("freq", None, None, "stn"),
        P(None, None, None, "stn"),
    )
    return jax.shard_map(
        local,
        mesh=mesh,
        in_specs=placed,
        out_specs=(
            P("freq", None, None, "stn"),
            P("freq", None, None, "stn"),
            P(None, None, None, "stn"),
        ),
        check_vma=False,
    )
```

time: 992 us -> 125 us (0.13); the launches traced: 980 us -> 124 us
  local copies, waits for them, and re-layouts: 416 us -> 1.07 us
  other arithmetic: 216 us -> 0 us
  waiting for transfers between devices: 142 us -> 12.2 us
  loops' own time: 85.4 us -> 0 us
  Pallas kernels: 0 us -> 66.7 us
  blocking collectives: 84.4 us -> 29.8 us
  matrix products: 20.2 us -> 0 us
  between operations: 16 us -> 0.66 us
  starting transfers between devices: 0.12 us -> 13.6 us
    slice x82 -> x0, local copies, waits for them, and re-layouts: 175 us -> none  [the longest x32 158 us: coherence(): far_imag = lax.dynamic_slice_in_dim(all_table[1], offset, block_span, 1)]
    psum x1 -> x0, waiting for transfers between devices: 91.9 us -> none  [local(): summed = lax.psum(weighted_sum, 'freq')]
    while x737 -> x0, local copies, waits for them, and re-layouts: 85.5 us -> none
    another operation x2 -> x0, loops' own time: 85.4 us -> none  [the longest x1 46.3 us: gradient_of(): lax.scan(gradient_direction_step, jnp.zeros((), jnp.float32), jnp.arange(...]
    pallas_call x0 -> x6, Pallas kernels: none -> 66.7 us  [the longest x1 31.5 us: local(): pl.pallas_call(model_kernel, grid=(STEPS,), in_specs=[pl.BlockSpec((SPAN,...]
    add x113 -> x0, other arithmetic: 59.4 us -> none  [the longest x16 36.9 us: residual_direction_step(): return (model_sum + pack_matrix(model_term), None)]
    dynamic_slice x97 -> x0, local copies, waits for them, and re-layouts: 58.9 us -> none  [the longest x32 29.4 us: residual_of(): lax.scan(residual_direction_step, jnp.zeros(band_vis.shape, jnp.float32),...]
    all_gather x1 -> x0, blocking collectives: 57.3 us -> none  [local(): all_gains = lax.all_gather(own_gains, 'stn', axis=2, tiled=True)]
  transfers between devices with their start and end apart: 3 -> 2, of which waited for: 2 -> 2; matrix products, arithmetic and copies ran while one was open for 3% -> 0% of each run, Pallas kernels for 0% -> 31%
where the time goes in v1:
time: 125 us; the launch traced here: 124 us
  Pallas kernels  66.7 us (53%)
  blocking collectives  29.8 us (24%)
  starting transfers between devices  13.6 us (11%)
  waiting for transfers between devices  12.2 us (10%)
    pallas_call x1, Pallas kernels, local(): pl.pallas_call(model_kernel, grid=(STEPS,), in_specs=[pl.BlockSpec((SPAN,...  31.5 us
    pallas_call x1, Pallas kernels, local(): pl.pallas_call(gradient_kernel, grid=(STEPS,), in_specs=[SMEM, SMEM, pl.B...  22.1 us
    all_to_all x1, blocking collectives, local(): gathered = lax.all_to_all(shared, 'freq', 0, 0, tiled=True)  17.4 us
    all_to_all x1, blocking collectives, local(): squares = lax.all_to_all(squares, 'stn', 0, 0, tiled=True)  12.4 us
    all_to_all x1, waiting for transfers between devices, local(): everyone = lax.all_to_all(copies, 'stn', 0, 0, tiled=True)  11.2 us
    all_to_all x1, starting transfers between devices, local(): everyone = lax.all_to_all(copies, 'stn', 0, 0, tiled=True)  9.98 us
    pallas_call x1, Pallas kernels, local(): pl.pallas_call(prepare_kernel, grid=(8,), in_specs=[SMEM, pl.BlockSpec((8...  7.5 us
    all_to_all x1, starting transfers between devices, local(): incoming = lax.all_to_all(outgoing, 'stn', 0, 0, tiled=True)  3.6 us
  transfers between devices with their start and end apart: 2, of which 2 were waited for; matrix products, arithmetic and copies ran while one was open for 0% of the time, Pallas kernels for 31%

profile of v1, /device:TPU:1, one launch (start us, length us, event | category | flops | bytes accessed | tf_op | source)
XLA Modules:
  0.0 124.0 jit_solution(16401369782141324215)
XLA Ops:
  0.6 1.8 %packet.1 = (f32[72,128]{1,0:T(8,128)}, f32[16,72,128]{2,1,0:T(8,128)}) custom-call(f32[8,16,64]{2,1,0:T(8,128)} %bitcast.18, f32[3,64]{1,0:T(4,128)} %stations_ref.1), custom_call_target="tpu_custom_call" | custom-call | tf_op jit(solution)/shard_map/packet/pallas_call | solution.py:438
  2.4 10.0 %all-to-all-start = ((f32[16,72,128]{2,1,0:T(8,128)}), f32[16,72,128]{2,1,0:T(8,128)S(1)}, u32[]{:S(2)}, u32[]{:S(2)}) async-start(f32[16,72,128]{2,1,0:T(8,128)} %get-tuple-element.17), calls=%async_computation | async-start | bytes 1179648 | tf_op jit(solution)/shard_map/all_to_all | solution.py:445
  12.4 7.5 %prepare.1 = (bf16[16,320,128]{2,1,0:T(8,128)(2,1)}, bf16[1536,128]{1,0:T(8,128)(2,1)}) custom-call(s32[1]{0:T(128)} %bitcast.band_ref, f32[8,64,1024]{2,1,0:T(8,128)} %bitcast.14, s32[64,1024]{1,0:T(8,128)} %mask_ref.3, f32[2,1536]{1,0:T(2,128)} %dirs_ref.1, f32[12,128]{1,0:T(8,128)} %bitcast.23, f32[2,1536]{1,0:T(2,128)} %pol_ref.1, f32[12,128]{1,0:T(8,128)} %bitcast.24, ...), custom_call_target="tpu_custom_call" | custom-call | flops 4000000000 | bytes 1000000 | tf_op jit(solution)/shard_map/prepare/pallas_call | solution.py:446
  19.9 11.2 %all-to-all-done.all_ref = f32[16,72,128]{2,1,0:T(8,128)S(1)} async-done(((f32[16,72,128]{2,1,0:T(8,128)}), f32[16,72,128]{2,1,0:T(8,128)S(1)}, u32[]{:S(2)}, u32[]{:S(2)}) %all-to-all-start) | async-done | bytes 589856 | tf_op jit(solution)/shard_map/all_to_all | solution.py:445
  31.0 0.0 copy-start.1
  31.0 3.6 %all-to-all-start.1 = ((bf16[16,320,128]{2,1,0:T(8,128)(2,1)}), bf16[16,320,128]{2,1,0:T(8,128)(2,1)S(1)}, u32[]{:S(2)}, u32[]{:S(2)}) async-start(bf16[16,320,128]{2,1,0:T(8,128)(2,1)} %get-tuple-element.21), calls=%async_computation.1 | async-start | bytes 2621440 | tf_op jit(solution)/shard_map/all_to_all | solution.py:470
  34.6 0.0 copy-done.1
  34.7 31.5 %model.1 = (bf16[4,1536,2048]{2,1,0:T(8,128)(2,1)}, bf16[6,1536,128]{2,1,0:T(8,128)(2,1)}, f32[256,2048]{1,0:T(8,128)}) custom-call(bf16[1536,128]{1,0:T(8,128)(2,1)} %get-tuple-element.16.sky_ref, f32[16,72,128]{2,1,0:T(8,128)} %copy-done.1, f32[72,128]{1,0:T(8,128)} %get-tuple-element.18.own_ref), custom_call_target="tpu_custom_call" | custom-call | flops 20000000000 | bytes 40000000 | tf_op jit(solution)/shard_map/model/pallas_call | solution.py:471
  66.1 1.1 all-to-all-done.1.got_ref
  67.2 0.0 copy-start
  67.2 1.1 copy-done
  68.3 22.1 %gradient.1 = (f32[64,128]{1,0:T(8,128)}, f32[16,128]{1,0:T(8,128)}) custom-call(s32[1]{0:T(128)} %bitcast.band_ref, s32[1]{0:T(128)} %bitcast.1.block_ref, bf16[4,1536,2048]{2,1,0:T(8,128)(2,1)} %get-tuple-element.19.far_ref, bf16[6,1536,128]{2,1,0:T(8,128)(2,1)} %get-tuple-element.20.weighted_ref, f32[8,64,1024]{2,1,0:T(8,128)} %bitcast.15, ...), custom_call_target="tpu_custom_call" | custom-call | flops 7000000000 | bytes 30000000 | tf_op jit(solution)/shard_map/gradient/pallas_call | solution.py:499
  90.3 12.4 %all_to_all.26 = f32[16,1,128]{2,1,0:T(1,128)} all-to-all(f32[16,1,128]{2,1,0:T(1,128)} %bitcast.20), channel_id=1, replica_groups=mesh['freq'=16,'stn'=16] {'stn'}, dimensions={0} | all-to-all | bytes 16384 | tf_op jit(solution)/shard_map/all_to_all | solution.py:520
  102.8 1.9 %update.1 = (f32[8,16,64]{2,1,0:T(8,128)}, f32[16,64,128]{2,1,0:T(8,128)}) custom-call(f32[16,128]{1,0:T(8,128)} %bitcast.19, f32[64,128]{1,0:T(8,128)} %get-tuple-element.24.drive_ref, f32[72,128]{1,0:T(8,128)} %get-tuple-element.18.own_ref, f32[8,16,64]{2,1,0:T(8,128)} %bitcast.17), custom_call_target="tpu_custom_call" | custom-call | tf_op jit(solution)/shard_map/update/pallas_call | solution.py:521
  104.6 17.4 %all_to_all.27.shared_ref = f32[16,64,128]{2,1,0:T(8,128)} all-to-all(f32[16,64,128]{2,1,0:T(8,128)} %get-tuple-element.26.own_ref), channel_id=1, replica_groups=mesh['freq'=16,'stn'=16] {'freq'}, dimensions={0} | all-to-all | bytes 1048576 | tf_op jit(solution)/shard_map/all_to_all | solution.py:528
  122.0 2.0 %finish.1 = (f32[8,16,64]{2,1,0:T(8,128)}, f32[4,8,16,64]{3,2,1,0:T(8,128)}) custom-call(s32[1]{0:T(128)} %bitcast.band_ref, f32[16,64,128]{2,1,0:T(8,128)} %all_to_all.27.shared_ref, f32[16,64,128]{2,1,0:T(8,128)} %get-tuple-element.26.own_ref), custom_call_target="tpu_custom_call" | custom-call | tf_op jit(solution)/shard_map/finish/pallas_call | solution.py:529
Async XLA Ops:
  2.4 28.6 %all-to-all-start = ((f32[16,72,128]{2,1,0:T(8,128)}), f32[16,72,128]{2,1,0:T(8,128)S(1)}, u32[]{:S(2)}, u32[]{:S(2)}) async-start(f32[16,72,128]{2,1,0:T(8,128)} %get-tuple-element.17), calls=%async_computation | async-start | bytes 1179648 | tf_op jit(solution)/shard_map/all_to_all | solution.py:445
  31.0 3.6 %copy-start.1 = (f32[16,72,128]{2,1,0:T(8,128)}, f32[16,72,128]{2,1,0:T(8,128)S(1)}, u32[]{:S(2)}) copy-start(f32[16,72,128]{2,1,0:T(8,128)S(1)} %all-to-all-done.all_ref) | copy-start | bytes 1769476
  31.0 36.2 %all-to-all-start.1 = ((bf16[16,320,128]{2,1,0:T(8,128)(2,1)}), bf16[16,320,128]{2,1,0:T(8,128)(2,1)S(1)}, u32[]{:S(2)}, u32[]{:S(2)}) async-start(bf16[16,320,128]{2,1,0:T(8,128)(2,1)} %get-tuple-element.21), calls=%async_computation.1 | async-start | bytes 2621440 | tf_op jit(solution)/shard_map/all_to_all | solution.py:470
  67.2 1.1 copy-start

commit v2 on v1

--- a/solution.py
+++ b/solution.py
@@ -19,7 +19,8 @@
 STEP_SIZE = 0.5
 F32 = jnp.float32
 BF16 = jnp.bfloat16
-SPAN = 128
+SPAN = 256
+CHUNK = 256
 STEPS = COMPS // SPAN
 VMEM = pl.BlockSpec(memory_space=pltpu.VMEM)
 SMEM = pl.BlockSpec(memory_space=pltpu.SMEM)
@@ -28,14 +29,15 @@
 def turn_polynomials():
     nodes = (np.cos(np.pi * (np.arange(64) + 0.5) / 64) + 1.0) / 8.0
     root = np.sqrt(nodes)
-    cos_fit = np.polynomial.Chebyshev.fit(nodes, np.cos(2 * np.pi * root), 6, domain=[0, 0.25])
-    sin_fit = np.polynomial.Chebyshev.fit(
-        nodes, -np.sin(2 * np.pi * root) / root, 5, domain=[0, 0.25]
-    )
-    to_list = lambda fit: [float(v) for v in fit.convert(kind=np.polynomial.Polynomial).coef]
-    return to_list(cos_fit), to_list(sin_fit)
-
-
+    scale = np.sqrt(2.0)
+    fits = []
+    for values in (scale * np.cos(np.pi * root), -scale * np.sin(np.pi * root) / root):
+        fit = np.polynomial.Chebyshev.fit(nodes, values, DEGREE, domain=[0, 0.25])
+        fits.append([float(v) for v in fit.convert(kind=np.polynomial.Polynomial).coef])
+    return fits
+
+
+DEGREE = 3
 COS_POLY, SIN_POLY = turn_polynomials()
 
 
@@ -62,8 +64,10 @@
 def phases(turns):
     frac = turns - jnp.floor(turns + 0.5)
     square = frac * frac
-    real = horner(COS_POLY, square)
-    imag = frac * horner(SIN_POLY, square)
+    half_cos = horner(COS_POLY, square)
+    half_sin = frac * horner(SIN_POLY, square)
+    real = 1.0 - half_sin * half_sin
+    imag = half_sin * half_cos
     return real.astype(BF16).astype(F32), imag.astype(BF16).astype(F32)
 
 
@@ -134,7 +138,12 @@
 
     for pair in range(4):
         put(pair, vis_ref[2 * pair] * mask, vis_ref[2 * pair + 1] * mask)
-    put(4, mask, mask)
+    lower = lax.broadcasted_iota(jnp.int32, (1, 128), 1) < 64
+    turned = jnp.concatenate([mask, mask], axis=0).T
+    for dest in range(2):
+        at = dest * 64
+        packed = jnp.where(lower, turned[at : at + 32], turned[at + 32 : at + 64])
+        out_ref[dest, 256:288, :] = packed.astype(BF16)
 
 
 def flat(ref):
@@ -197,7 +206,7 @@
 
 
 def model_kernel(
-    sky_ref, all_ref, own_ref, far_ref, weighted_ref, model_ref, geo_ref, geo_own_ref, gains_ref, turns_ref
+    sky_ref, all_ref, own_ref, far_ref, weighted_ref, model_ref, geo_ref, geo_own_ref, gains_ref
 ):
     step = pl.program_id(0)
     lower = lax.broadcasted_iota(jnp.int32, (1, 128), 1) < 64
@@ -216,25 +225,6 @@
             gains_ref[:, 1024 + tile * 128 : 1024 + tile * 128 + 128] = high_part
 
     sky = sky_ref[...]
-    turns_ref[...] = jnp.dot(sky, geo_ref[...], preferred_element_type=F32)
-
-    def rows_step(at, carry):
-        rows = pl.ds(pl.multiple_of(at * 16, 16), 16)
-        for lane in range(0, NS, 256):
-            real, imag = phases(turns_ref[rows, lane : lane + 256])
-            for row in range(2):
-                lanes = slice(row * NS + lane, row * NS + lane + 256)
-                for column in range(2):
-                    gain_re = gains_ref[column * 32 : column * 32 + 16, lanes]
-                    gain_im = gains_ref[column * 32 + 16 : column * 32 + 32, lanes]
-                    far_ref[column, rows, lanes] = (real * gain_re - imag * gain_im).astype(BF16)
-                    far_ref[2 + column, rows, lanes] = (real * gain_im + imag * gain_re).astype(
-                        BF16
-                    )
-        return carry
-
-    lax.fori_loop(0, SPAN // 16, rows_step, 0)
-
     own_re, own_im = phases(jnp.dot(sky, geo_own_ref[...], preferred_element_type=F32))
     source = lax.broadcasted_iota(jnp.int32, (128, 384), 0)
     target = 3 + lax.broadcasted_iota(jnp.int32, (128, 384), 1) // 128
@@ -247,7 +237,7 @@
         weighted_ref[2 * flux] = pair[0]
         weighted_ref[2 * flux + 1] = pair[1]
         weighted.append((pair[0].astype(F32), pair[1].astype(F32)))
-    gains = [jnp.concatenate([own_ref[at * 16 : at * 16 + 16]] * 8, axis=0) for at in range(4)]
+    gains = [jnp.concatenate([own_ref[at * 16 : at * 16 + 16]] * (SPAN // 16), axis=0) for at in range(4)]
     near_re, near_im = [], []
     for first, second in ((0, 1), (1, 2)):
         (ar, ai), (br, bi) = weighted[first], weighted[second]
@@ -262,8 +252,26 @@
         ],
         axis=0,
     ).astype(BF16)
-    far = far_ref[...].reshape(4 * SPAN, 2 * NS)
-    model_ref[...] += jnp.dot(near, far, preferred_element_type=F32)
+    for lane in range(0, NS, CHUNK):
+        turns = jnp.dot(
+            sky, geo_ref[:, lane : lane + CHUNK], preferred_element_type=F32
+        )
+        for at in range(0, SPAN, 16):
+            rows = slice(at, at + 16)
+            real, imag = phases(turns[rows])
+            for row in range(2):
+                lanes = slice(row * NS + lane, row * NS + lane + CHUNK)
+                for column in range(2):
+                    gain_re = gains_ref[column * 32 : column * 32 + 16, lanes]
+                    gain_im = gains_ref[column * 32 + 16 : column * 32 + 32, lanes]
+                    far_ref[column, rows, lanes] = (real * gain_re - imag * gain_im).astype(BF16)
+                    far_ref[2 + column, rows, lanes] = (real * gain_im + imag * gain_re).astype(
+                        BF16
+                    )
+        for row in range(2):
+            lanes = slice(row * NS + lane, row * NS + lane + CHUNK)
+            far = far_ref[:, :, lanes].reshape(4 * SPAN, CHUNK)
+            model_ref[:, lanes] += jnp.dot(near, far, preferred_element_type=F32)
 
 
 def gradient_kernel(
@@ -283,6 +291,7 @@
     both_ref,
     near_ref,
     sum_ref,
+    turned_ref,
 ):
     step = pl.program_id(0)
     own_tile = block_ref[0] // 2
@@ -291,42 +300,43 @@
     def _():
         sum_ref[...] = jnp.zeros_like(sum_ref)
         lower = lax.broadcasted_iota(jnp.int32, (1, 128), 1) < 64
-        for tile in range(8):
-            lanes = slice(tile * 128, tile * 128 + 128)
+
+        def both_sides(tile, lane):
+            lanes = pl.ds(lane, 128)
+            far_lanes = pl.ds(NS + lane, 128)
             mask = mask_ref[:, lanes].astype(F32)
 
-            def halves(pair):
-                first = got_ref[2 * tile, pair * 64 : pair * 64 + 64, :].astype(F32)
-                second = got_ref[2 * tile + 1, pair * 64 : pair * 64 + 64, :].astype(F32)
-                return first, second
-
-            first, second = halves(4)
-            mask_both = mask + jnp.where(lower, first, second)
+            def halves(top, count):
+                first = got_ref[2 * tile, top : top + count, :].astype(F32)
+                second = got_ref[2 * tile + 1, top : top + count, :].astype(F32)
+                return (
+                    jnp.where(lower, first, pltpu.roll(second, 64, 1)),
+                    jnp.where(lower, pltpu.roll(first, 64, 1), second),
+                )
+
+            mask_both = mask + jnp.concatenate(halves(256, 32), axis=0)
             for row in range(2):
                 for column in range(2):
-                    first, second = halves(2 * column + row)
-                    real = jnp.where(lower, first, pltpu.roll(second, 64, 1))
-                    imag = jnp.where(lower, pltpu.roll(first, 64, 1), second)
-                    at = column * NS + tile * 128
+                    real, imag = halves((2 * column + row) * 64, 64)
                     for part, other in ((0, real), (1, -imag)):
                         top = part * 128 + row * 64
                         vis = vis_ref[4 * row + 2 * column + part, :, lanes]
-                        model = model_ref[top : top + 64, at : at + 128]
-                        value = vis * mask + other - mask_both * model
-                        high = value.astype(BF16)
-                        both_ref[top : top + 64, at : at + 128] = high
-
-                        @pl.when(tile == own_tile)
-                        def _(value=value, high=high, top=top, column=column):
-                            near_ref[top : top + 64, column * 128 : column * 128 + 128] = (
-                                value - high.astype(F32)
-                            ).astype(BF16)
-
-    product = lax.dot_general(
-        far_ref[...].reshape(4 * SPAN, 2 * NS),
-        both_ref[...],
-        (((1,), (1,)), ((), ())),
-        preferred_element_type=F32,
+                        model = model_ref[top : top + 64, far_lanes if column else lanes]
+                        yield top, column, vis * mask + other - mask_both * model
+
+        for tile in range(8):
+            for top, column, value in both_sides(tile, tile * 128):
+                at = column * NS + tile * 128
+                both_ref[top : top + 64, at : at + 128] = value.astype(BF16)
+        for top, column, value in both_sides(own_tile, pl.multiple_of(own_tile * 128, 128)):
+            near_ref[top : top + 64, column * 128 : column * 128 + 128] = (
+                value - value.astype(BF16).astype(F32)
+            ).astype(BF16)
+        for lane in range(0, 2 * NS, 256):
+            turned_ref[lane : lane + 256, :] = both_ref[:, lane : lane + 256].T
+
+    product = jnp.dot(
+        far_ref[...].reshape(4 * SPAN, 2 * NS), turned_ref[...], preferred_element_type=F32
     )
     lane = pl.multiple_of(own_tile * 128, 128)
     beside = jnp.concatenate(
@@ -417,6 +427,65 @@
     return pl.CostEstimate(flops=int(flops), bytes_accessed=int(moved), transcendentals=0)
 
 
+BIG = pltpu.CompilerParams(vmem_limit_bytes=56 * 1024 * 1024)
+shape = jax.ShapeDtypeStruct
+
+
+def call_model(sky, everyone, own):
+    return pl.pallas_call(
+        model_kernel,
+        grid=(STEPS,),
+        in_specs=[
+            pl.BlockSpec((SPAN, 128), lambda at: (at, 0)),
+            VMEM,
+            VMEM,
+        ],
+        out_specs=[
+            pl.BlockSpec((4, SPAN, 2 * NS), lambda at: (0, at, 0)),
+            pl.BlockSpec((6, SPAN, 128), lambda at: (0, at, 0)),
+            pl.BlockSpec((256, 2 * NS), lambda at: (0, 0)),
+        ],
+        out_shape=[
+            shape((4, COMPS, 2 * NS), BF16),
+            shape((6, COMPS, 128), BF16),
+            shape((256, 2 * NS), F32),
+        ],
+        scratch_shapes=[
+            pltpu.VMEM((128, NS), BF16),
+            pltpu.VMEM((128, 128), BF16),
+            pltpu.VMEM((64, 2 * NS), F32),
+        ],
+        compiler_params=BIG,
+        cost_estimate=cost(2e10, 4e7),
+        name="model",
+    )(sky, everyone, own)
+
+
+def call_gradient(*operands):
+    return pl.pallas_call(
+        gradient_kernel,
+        grid=(STEPS,),
+        in_specs=[
+            SMEM,
+            SMEM,
+            pl.BlockSpec((4, SPAN, 2 * NS), lambda at: (0, at, 0)),
+            pl.BlockSpec((6, SPAN, 128), lambda at: (0, at, 0)),
+        ]
+        + [VMEM] * 7,
+        out_specs=[VMEM, VMEM],
+        out_shape=[shape((64, 128), F32), shape((BLOCKS, 128), F32)],
+        scratch_shapes=[
+            pltpu.VMEM((256, 2 * NS), BF16),
+            pltpu.VMEM((256, 256), BF16),
+            pltpu.VMEM((64, 128), F32),
+            pltpu.VMEM((2 * NS, 256), BF16),
+        ],
+        compiler_params=BIG,
+        cost_estimate=cost(7e9, 3e7),
+        name="gradient",
+    )(*operands)
+
+
 def local(
     visibilities,
     flag_mask,
@@ -433,8 +502,6 @@
     band = lax.axis_index("freq").reshape(1).astype(jnp.int32)
     block = lax.axis_index("stn").reshape(1).astype(jnp.int32)
     vis, jones, duals = visibilities[0], jones_gains[0], scaled_duals[0]
-    shape = jax.ShapeDtypeStruct
-    big = pltpu.CompilerParams(vmem_limit_bytes=56 * 1024 * 1024)
     own, copies = pl.pallas_call(
         packet_kernel,
         out_shape=[shape((72, 128), F32), shape((BLOCKS, 72, 128), F32)],
@@ -452,9 +519,9 @@
             pl.BlockSpec((OWN, 128), lambda at: (0, at)),
         ]
         + [VMEM] * 5,
-        out_specs=[pl.BlockSpec((2, 320, 128), lambda at: (at, 0, 0)), VMEM],
-        out_shape=[shape((BLOCKS, 320, 128), BF16), shape((COMPS, 128), BF16)],
-        compiler_params=big,
+        out_specs=[pl.BlockSpec((2, 288, 128), lambda at: (at, 0, 0)), VMEM],
+        out_shape=[shape((BLOCKS, 288, 128), BF16), shape((COMPS, 128), BF16)],
+        compiler_params=BIG,
         cost_estimate=cost(4e9, 1e6),
         name="prepare",
     )(
@@ -468,55 +535,10 @@
         clusters.reshape(COMPS // 128, 128),
     )
     incoming = lax.all_to_all(outgoing, "stn", 0, 0, tiled=True)
-    far, weighted, model = pl.pallas_call(
-        model_kernel,
-        grid=(STEPS,),
-        in_specs=[
-            pl.BlockSpec((SPAN, 128), lambda at: (at, 0)),
-            VMEM,
-            VMEM,
-        ],
-        out_specs=[
-            pl.BlockSpec((4, SPAN, 2 * NS), lambda at: (0, at, 0)),
-            pl.BlockSpec((6, SPAN, 128), lambda at: (0, at, 0)),
-            pl.BlockSpec((256, 2 * NS), lambda at: (0, 0)),
-        ],
-        out_shape=[
-            shape((4, COMPS, 2 * NS), BF16),
-            shape((6, COMPS, 128), BF16),
-            shape((256, 2 * NS), F32),
-        ],
-        scratch_shapes=[
-            pltpu.VMEM((128, NS), BF16),
-            pltpu.VMEM((128, 128), BF16),
-            pltpu.VMEM((64, 2 * NS), F32),
-            pltpu.VMEM((SPAN, NS), F32),
-        ],
-        compiler_params=big,
-        cost_estimate=cost(2e10, 4e7),
-        name="model",
-    )(sky, everyone, own)
-    drive, squares = pl.pallas_call(
-        gradient_kernel,
-        grid=(STEPS,),
-        in_specs=[
-            SMEM,
-            SMEM,
-            pl.BlockSpec((4, SPAN, 2 * NS), lambda at: (0, at, 0)),
-            pl.BlockSpec((6, SPAN, 128), lambda at: (0, at, 0)),
-        ]
-        + [VMEM] * 7,
-        out_specs=[VMEM, VMEM],
-        out_shape=[shape((64, 128), F32), shape((BLOCKS, 128), F32)],
-        scratch_shapes=[
-            pltpu.VMEM((256, 2 * NS), BF16),
-            pltpu.VMEM((256, 256), BF16),
-            pltpu.VMEM((64, 128), F32),
-        ],
-        compiler_params=big,
-        cost_estimate=cost(7e9, 3e7),
-        name="gradient",
-    )(band, block, far, weighted, vis, flag_mask, incoming, model, own, duals, consensus)
+    far, weighted, model = call_model(sky, everyone, own)
+    drive, squares = call_gradient(
+        band, block, far, weighted, vis, flag_mask, incoming, model, own, duals, consensus
+    )
     squares = lax.all_to_all(squares, "stn", 0, 0, tiled=True)
     jones_next, shared = pl.pallas_call(
         update_kernel,

time: 125 us -> 115 us (0.920)
  Pallas kernels: 66.7 us -> 55.3 us
  waiting for transfers between devices: 12.2 us -> 15.9 us
  blocking collectives: 29.8 us -> 28 us
    pallas_call x2, Pallas kernels: 53.6 us -> 42.1 us  [the longest x1 25.3 us: call_model(): pl.pallas_call(model_kernel, grid=(STEPS,), in_specs=[pl.BlockSpec((SPAN,...]
    all_to_all x1, waiting for transfers between devices: 1.07 us -> 4.66 us  [local(): incoming = lax.all_to_all(outgoing, 'stn', 0, 0, tiled=True)]
    all_to_all x1, blocking collectives: 12.4 us -> 10.6 us  [local(): squares = lax.all_to_all(squares, 'stn', 0, 0, tiled=True)]
  transfers between devices with their start and end apart: 2 -> 2, of which waited for: 2 -> 2; matrix products, arithmetic and copies ran while one was open for 0% -> 0% of each run, Pallas kernels for 31% -> 29%
where the time goes in v2:
time: 115 us; the launch traced here: 114 us
  Pallas kernels  55.3 us (48%)
  blocking collectives  28 us (24%)
  waiting for transfers between devices  15.9 us (14%)
  starting transfers between devices  13.6 us (12%)
    pallas_call x1, Pallas kernels, call_model(): pl.pallas_call(model_kernel, grid=(STEPS,), in_specs=[pl.BlockSpec((SPAN,...  25.3 us
    all_to_all x1, blocking collectives, local(): gathered = lax.all_to_all(shared, 'freq', 0, 0, tiled=True)  17.4 us
    pallas_call x1, Pallas kernels, call_gradient(): pl.pallas_call(gradient_kernel, grid=(STEPS,), in_specs=[SMEM, SMEM, pl.B...  16.9 us
    all_to_all x1, waiting for transfers between devices, local(): everyone = lax.all_to_all(copies, 'stn', 0, 0, tiled=True)  11.2 us
    all_to_all x1, blocking collectives, local(): squares = lax.all_to_all(squares, 'stn', 0, 0, tiled=True)  10.6 us
    all_to_all x1, starting transfers between devices, local(): everyone = lax.all_to_all(copies, 'stn', 0, 0, tiled=True)  9.98 us
    pallas_call x1, Pallas kernels, local(): pl.pallas_call(prepare_kernel, grid=(8,), in_specs=[SMEM, pl.BlockSpec((8...  7.47 us
    all_to_all x1, waiting for transfers between devices, local(): incoming = lax.all_to_all(outgoing, 'stn', 0, 0, tiled=True)  4.66 us
  transfers between devices with their start and end apart: 2, of which 2 were waited for; matrix products, arithmetic and copies ran while one was open for 0% of the time, Pallas kernels for 29%

profile of v2, /device:TPU:1, one launch (start us, length us, event | category | flops | bytes accessed | tf_op | source)
XLA Modules:
  0.0 114.4 jit_solution(533657050806229967)
XLA Ops:
  0.6 1.8 %packet.1 = (f32[72,128]{1,0:T(8,128)}, f32[16,72,128]{2,1,0:T(8,128)}) custom-call(f32[8,16,64]{2,1,0:T(8,128)} %bitcast.18, f32[3,64]{1,0:T(4,128)} %stations_ref.1), custom_call_target="tpu_custom_call" | custom-call | tf_op jit(solution)/shard_map/packet/pallas_call | solution.py:505
  2.4 10.0 %all-to-all-start = ((f32[16,72,128]{2,1,0:T(8,128)}), f32[16,72,128]{2,1,0:T(8,128)S(1)}, u32[]{:S(2)}, u32[]{:S(2)}) async-start(f32[16,72,128]{2,1,0:T(8,128)} %get-tuple-element.17), calls=%async_computation | async-start | bytes 1179648 | tf_op jit(solution)/shard_map/all_to_all | solution.py:512
  12.4 7.5 %prepare.1 = (bf16[16,288,128]{2,1,0:T(8,128)(2,1)}, bf16[1536,128]{1,0:T(8,128)(2,1)}) custom-call(s32[1]{0:T(128)} %bitcast.band_ref, f32[8,64,1024]{2,1,0:T(8,128)} %bitcast.14, s32[64,1024]{1,0:T(8,128)} %mask_ref.3, f32[2,1536]{1,0:T(2,128)} %dirs_ref.1, f32[12,128]{1,0:T(8,128)} %bitcast.23, f32[2,1536]{1,0:T(2,128)} %pol_ref.1, f32[12,128]{1,0:T(8,128)} %bitcast.24, ...), custom_call_target="tpu_custom_call" | custom-call | flops 4000000000 | bytes 1000000 | tf_op jit(solution)/shard_map/prepare/pallas_call | solution.py:513
  19.8 11.2 %all-to-all-done.all_ref = f32[16,72,128]{2,1,0:T(8,128)S(1)} async-done(((f32[16,72,128]{2,1,0:T(8,128)}), f32[16,72,128]{2,1,0:T(8,128)S(1)}, u32[]{:S(2)}, u32[]{:S(2)}) %all-to-all-start) | async-done | bytes 589856 | tf_op jit(solution)/shard_map/all_to_all | solution.py:512
  31.0 0.0 copy-start.1
  31.0 3.6 %all-to-all-start.1 = ((bf16[16,288,128]{2,1,0:T(8,128)(2,1)}), bf16[16,288,128]{2,1,0:T(8,128)(2,1)S(1)}, u32[]{:S(2)}, u32[]{:S(2)}) async-start(bf16[16,288,128]{2,1,0:T(8,128)(2,1)} %get-tuple-element.21), calls=%async_computation.1 | async-start | bytes 2359296 | tf_op jit(solution)/shard_map/all_to_all | solution.py:537
  34.6 0.0 copy-done.1
  34.7 25.3 %model.1 = (bf16[4,1536,2048]{2,1,0:T(8,128)(2,1)}, bf16[6,1536,128]{2,1,0:T(8,128)(2,1)}, f32[256,2048]{1,0:T(8,128)}) custom-call(bf16[1536,128]{1,0:T(8,128)(2,1)} %get-tuple-element.16.sky_ref, f32[16,72,128]{2,1,0:T(8,128)} %copy-done.1, f32[72,128]{1,0:T(8,128)} %get-tuple-element.18.own_ref), custom_call_target="tpu_custom_call" | custom-call | flops 20000000000 | bytes 40000000 | tf_op jit(solution)/shard_map/model/pallas_call | solution.py:435
  59.9 4.7 %all-to-all-done.1.got_ref = bf16[16,288,128]{2,1,0:T(8,128)(2,1)S(1)} async-done(((bf16[16,288,128]{2,1,0:T(8,128)(2,1)}), bf16[16,288,128]{2,1,0:T(8,128)(2,1)S(1)}, u32[]{:S(2)}, u32[]{:S(2)}) %all-to-all-start.1) | async-done | bytes 1179680 | tf_op jit(solution)/shard_map/all_to_all | solution.py:537
  64.6 0.0 copy-start
  64.6 1.1 copy-done
  65.6 16.9 %gradient.1 = (f32[64,128]{1,0:T(8,128)}, f32[16,128]{1,0:T(8,128)}) custom-call(s32[1]{0:T(128)} %bitcast.band_ref, s32[1]{0:T(128)} %bitcast.1.block_ref, bf16[4,1536,2048]{2,1,0:T(8,128)(2,1)} %get-tuple-element.19.far_ref, bf16[6,1536,128]{2,1,0:T(8,128)(2,1)} %get-tuple-element.20.weighted_ref, f32[8,64,1024]{2,1,0:T(8,128)} %bitcast.15, ...), custom_call_target="tpu_custom_call" | custom-call | flops 7000000000 | bytes 30000000 | tf_op jit(solution)/shard_map/gradient/pallas_call | solution.py:465
  82.5 10.6 %all_to_all.26 = f32[16,1,128]{2,1,0:T(1,128)} all-to-all(f32[16,1,128]{2,1,0:T(1,128)} %bitcast.20), channel_id=1, replica_groups=mesh['freq'=16,'stn'=16] {'stn'}, dimensions={0} | all-to-all | bytes 16384 | tf_op jit(solution)/shard_map/all_to_all | solution.py:542
  93.1 1.9 %update.1 = (f32[8,16,64]{2,1,0:T(8,128)}, f32[16,64,128]{2,1,0:T(8,128)}) custom-call(f32[16,128]{1,0:T(8,128)} %bitcast.19, f32[64,128]{1,0:T(8,128)} %get-tuple-element.24.drive_ref, f32[72,128]{1,0:T(8,128)} %get-tuple-element.18.own_ref, f32[8,16,64]{2,1,0:T(8,128)} %bitcast.17), custom_call_target="tpu_custom_call" | custom-call | tf_op jit(solution)/shard_map/update/pallas_call | solution.py:543
  95.0 17.4 %all_to_all.27.shared_ref = f32[16,64,128]{2,1,0:T(8,128)} all-to-all(f32[16,64,128]{2,1,0:T(8,128)} %get-tuple-element.26.own_ref), channel_id=1, replica_groups=mesh['freq'=16,'stn'=16] {'freq'}, dimensions={0} | all-to-all | bytes 1048576 | tf_op jit(solution)/shard_map/all_to_all | solution.py:550
  112.4 2.0 %finish.1 = (f32[8,16,64]{2,1,0:T(8,128)}, f32[4,8,16,64]{3,2,1,0:T(8,128)}) custom-call(s32[1]{0:T(128)} %bitcast.band_ref, f32[16,64,128]{2,1,0:T(8,128)} %all_to_all.27.shared_ref, f32[16,64,128]{2,1,0:T(8,128)} %get-tuple-element.26.own_ref), custom_call_target="tpu_custom_call" | custom-call | tf_op jit(solution)/shard_map/finish/pallas_call | solution.py:551
Async XLA Ops:
  2.4 28.6 %all-to-all-start = ((f32[16,72,128]{2,1,0:T(8,128)}), f32[16,72,128]{2,1,0:T(8,128)S(1)}, u32[]{:S(2)}, u32[]{:S(2)}) async-start(f32[16,72,128]{2,1,0:T(8,128)} %get-tuple-element.17), calls=%async_computation | async-start | bytes 1179648 | tf_op jit(solution)/shard_map/all_to_all | solution.py:512
  31.0 3.6 %copy-start.1 = (f32[16,72,128]{2,1,0:T(8,128)}, f32[16,72,128]{2,1,0:T(8,128)S(1)}, u32[]{:S(2)}) copy-start(f32[16,72,128]{2,1,0:T(8,128)S(1)} %all-to-all-done.all_ref) | copy-start | bytes 1769476
  31.0 33.5 %all-to-all-start.1 = ((bf16[16,288,128]{2,1,0:T(8,128)(2,1)}), bf16[16,288,128]{2,1,0:T(8,128)(2,1)S(1)}, u32[]{:S(2)}, u32[]{:S(2)}) async-start(bf16[16,288,128]{2,1,0:T(8,128)(2,1)} %get-tuple-element.21), calls=%async_computation.1 | async-start | bytes 2359296 | tf_op jit(solution)/shard_map/all_to_all | solution.py:537
  64.6 1.1 copy-start

commit v3 on v2

--- a/solution.py
+++ b/solution.py
@@ -19,7 +19,7 @@
 STEP_SIZE = 0.5
 F32 = jnp.float32
 BF16 = jnp.bfloat16
-SPAN = 256
+SPAN = 384
 CHUNK = 256
 STEPS = COMPS // SPAN
 VMEM = pl.BlockSpec(memory_space=pltpu.VMEM)
@@ -427,7 +427,7 @@
     return pl.CostEstimate(flops=int(flops), bytes_accessed=int(moved), transcendentals=0)
 
 
-BIG = pltpu.CompilerParams(vmem_limit_bytes=56 * 1024 * 1024)
+BIG = pltpu.CompilerParams(vmem_limit_bytes=54 * 1024 * 1024)
 shape = jax.ShapeDtypeStruct
 
 
@@ -535,9 +535,10 @@
         clusters.reshape(COMPS // 128, 128),
     )
     incoming = lax.all_to_all(outgoing, "stn", 0, 0, tiled=True)
+    incoming = pltpu.with_memory_space_constraint(incoming, pltpu.VMEM)
     far, weighted, model = call_model(sky, everyone, own)
     drive, squares = call_gradient(
-        band, block, far, weighted, vis, flag_mask, incoming, model, own, duals, consensus
+        band, block, far, weighted, pltpu.with_memory_space_constraint(vis, pltpu.VMEM), flag_mask, incoming, model, own, duals, consensus
     )
     squares = lax.all_to_all(squares, "stn", 0, 0, tiled=True)
     jones_next, shared = pl.pallas_call(

time: 115 us -> 113 us (0.983)
  Pallas kernels: 55.3 us -> 53 us
    pallas_call x1, Pallas kernels: 16.9 us -> 15.4 us  [call_gradient(): pl.pallas_call(gradient_kernel, grid=(STEPS,), in_specs=[SMEM, SMEM, pl.B...]
  transfers between devices with their start and end apart: 2 -> 2, of which waited for: 2 -> 2; matrix products, arithmetic and copies ran while one was open for 0% -> 0% of each run, Pallas kernels for 29% -> 28%
where the time goes in v3:
time: 113 us
  Pallas kernels  53 us (47%)
  blocking collectives  28 us (25%)
  waiting for transfers between devices  16.6 us (15%)
  starting transfers between devices  13.6 us (12%)
    pallas_call x1, Pallas kernels, call_model(): pl.pallas_call(model_kernel, grid=(STEPS,), in_specs=[pl.BlockSpec((SPAN,...  24.5 us
    all_to_all x1, blocking collectives, local(): gathered = lax.all_to_all(shared, 'freq', 0, 0, tiled=True)  17.4 us
    pallas_call x1, Pallas kernels, call_gradient(): pl.pallas_call(gradient_kernel, grid=(STEPS,), in_specs=[SMEM, SMEM, pl.B...  15.4 us
    all_to_all x1, waiting for transfers between devices, local(): everyone = lax.all_to_all(copies, 'stn', 0, 0, tiled=True)  11.2 us
    all_to_all x1, blocking collectives, local(): squares = lax.all_to_all(squares, 'stn', 0, 0, tiled=True)  10.6 us
    all_to_all x1, starting transfers between devices, local(): everyone = lax.all_to_all(copies, 'stn', 0, 0, tiled=True)  9.98 us
    pallas_call x1, Pallas kernels, local(): pl.pallas_call(prepare_kernel, grid=(8,), in_specs=[SMEM, pl.BlockSpec((8...  7.47 us
    all_to_all x1, waiting for transfers between devices, local(): incoming = lax.all_to_all(outgoing, 'stn', 0, 0, tiled=True)  5.37 us
  transfers between devices with their start and end apart: 2, of which 2 were waited for; matrix products, arithmetic and copies ran while one was open for 0% of the time, Pallas kernels for 28%

profile of v3, /device:TPU:1, one launch (start us, length us, event | category | flops | bytes accessed | tf_op | source)
XLA Modules:
  0.0 112.6 jit_solution(11912646430704827517)
XLA Ops:
  0.6 1.8 %packet.1 = (f32[72,128]{1,0:T(8,128)}, f32[16,72,128]{2,1,0:T(8,128)}) custom-call(f32[8,16,64]{2,1,0:T(8,128)} %bitcast.18, f32[3,64]{1,0:T(4,128)} %stations_ref.1), custom_call_target="tpu_custom_call" | custom-call | tf_op jit(solution)/shard_map/packet/pallas_call | solution.py:505
  2.4 10.0 %all-to-all-start = ((f32[16,72,128]{2,1,0:T(8,128)}), f32[16,72,128]{2,1,0:T(8,128)S(1)}, u32[]{:S(2)}, u32[]{:S(2)}) async-start(f32[16,72,128]{2,1,0:T(8,128)} %get-tuple-element.17), calls=%async_computation | async-start | bytes 1179648 | tf_op jit(solution)/shard_map/all_to_all | solution.py:512
  12.4 7.5 %prepare.1 = (bf16[16,288,128]{2,1,0:T(8,128)(2,1)}, bf16[1536,128]{1,0:T(8,128)(2,1)}) custom-call(s32[1]{0:T(128)} %bitcast.band_ref, f32[8,64,1024]{2,1,0:T(8,128)} %bitcast.14, s32[64,1024]{1,0:T(8,128)} %mask_ref.3, f32[2,1536]{1,0:T(2,128)} %dirs_ref.1, f32[12,128]{1,0:T(8,128)} %bitcast.23, f32[2,1536]{1,0:T(2,128)} %pol_ref.1, f32[12,128]{1,0:T(8,128)} %bitcast.24, ...), custom_call_target="tpu_custom_call" | custom-call | flops 4000000000 | bytes 1000000 | tf_op jit(solution)/shard_map/prepare/pallas_call | solution.py:513
  19.8 11.2 %all-to-all-done.all_ref = f32[16,72,128]{2,1,0:T(8,128)S(1)} async-done(((f32[16,72,128]{2,1,0:T(8,128)}), f32[16,72,128]{2,1,0:T(8,128)S(1)}, u32[]{:S(2)}, u32[]{:S(2)}) %all-to-all-start) | async-done | bytes 589856 | tf_op jit(solution)/shard_map/all_to_all | solution.py:512
  31.0 0.0 copy-start.1
  31.0 0.8 copy-done.1
  31.8 3.6 %all-to-all-start.1 = ((bf16[16,288,128]{2,1,0:T(8,128)(2,1)}), bf16[16,288,128]{2,1,0:T(8,128)(2,1)S(1)}, u32[]{:S(2)}, u32[]{:S(2)}) async-start(bf16[16,288,128]{2,1,0:T(8,128)(2,1)} %get-tuple-element.21), calls=%async_computation.1 | async-start | bytes 2359296 | tf_op jit(solution)/shard_map/all_to_all | solution.py:537
  35.4 0.0 copy-start
  35.5 24.5 %model.1 = (bf16[4,1536,2048]{2,1,0:T(8,128)(2,1)}, bf16[6,1536,128]{2,1,0:T(8,128)(2,1)}, f32[256,2048]{1,0:T(8,128)}) custom-call(bf16[1536,128]{1,0:T(8,128)(2,1)} %get-tuple-element.16.sky_ref, f32[16,72,128]{2,1,0:T(8,128)} %copy-done.1, f32[72,128]{1,0:T(8,128)} %get-tuple-element.18.own_ref), custom_call_target="tpu_custom_call" | custom-call | flops 20000000000 | bytes 40000000 | tf_op jit(solution)/shard_map/model/pallas_call | solution.py:435
  60.0 5.4 %all-to-all-done.1.got_ref = bf16[16,288,128]{2,1,0:T(8,128)(2,1)S(1)} async-done(((bf16[16,288,128]{2,1,0:T(8,128)(2,1)}), bf16[16,288,128]{2,1,0:T(8,128)(2,1)S(1)}, u32[]{:S(2)}, u32[]{:S(2)}) %all-to-all-start.1) | async-done | bytes 1179680 | tf_op jit(solution)/shard_map/all_to_all | solution.py:537
  65.4 0.0 copy-done
  65.4 15.4 %gradient.1 = (f32[64,128]{1,0:T(8,128)}, f32[16,128]{1,0:T(8,128)}) custom-call(s32[1]{0:T(128)} %bitcast.band_ref, s32[1]{0:T(128)} %bitcast.1.block_ref, bf16[4,1536,2048]{2,1,0:T(8,128)(2,1)} %get-tuple-element.19.far_ref, bf16[6,1536,128]{2,1,0:T(8,128)(2,1)} %get-tuple-element.20.weighted_ref, f32[8,64,1024]{2,1,0:T(8,128)S(1)} %bitcast.15, ...), custom_call_target="tpu_custom_call" | custom-call | flops 7000000000 | bytes 30000000 | tf_op jit(solution)/shard_map/gradient/pallas_call | solution.py:465
  80.7 10.6 %all_to_all.26 = f32[16,1,128]{2,1,0:T(1,128)} all-to-all(f32[16,1,128]{2,1,0:T(1,128)} %bitcast.20), channel_id=1, replica_groups=mesh['freq'=16,'stn'=16] {'stn'}, dimensions={0} | all-to-all | bytes 16384 | tf_op jit(solution)/shard_map/all_to_all | solution.py:543
  91.3 1.9 %update.1 = (f32[8,16,64]{2,1,0:T(8,128)}, f32[16,64,128]{2,1,0:T(8,128)}) custom-call(f32[16,128]{1,0:T(8,128)} %bitcast.19, f32[64,128]{1,0:T(8,128)} %get-tuple-element.24.drive_ref, f32[72,128]{1,0:T(8,128)} %get-tuple-element.18.own_ref, f32[8,16,64]{2,1,0:T(8,128)} %bitcast.17), custom_call_target="tpu_custom_call" | custom-call | tf_op jit(solution)/shard_map/update/pallas_call | solution.py:544
  93.2 17.4 %all_to_all.27.shared_ref = f32[16,64,128]{2,1,0:T(8,128)} all-to-all(f32[16,64,128]{2,1,0:T(8,128)} %get-tuple-element.26.own_ref), channel_id=1, replica_groups=mesh['freq'=16,'stn'=16] {'freq'}, dimensions={0} | all-to-all | bytes 1048576 | tf_op jit(solution)/shard_map/all_to_all | solution.py:551
  110.6 2.0 %finish.1 = (f32[8,16,64]{2,1,0:T(8,128)}, f32[4,8,16,64]{3,2,1,0:T(8,128)}) custom-call(s32[1]{0:T(128)} %bitcast.band_ref, f32[16,64,128]{2,1,0:T(8,128)} %all_to_all.27.shared_ref, f32[16,64,128]{2,1,0:T(8,128)} %get-tuple-element.26.own_ref), custom_call_target="tpu_custom_call" | custom-call | tf_op jit(solution)/shard_map/finish/pallas_call | solution.py:552
Async XLA Ops:
  2.4 28.6 %all-to-all-start = ((f32[16,72,128]{2,1,0:T(8,128)}), f32[16,72,128]{2,1,0:T(8,128)S(1)}, u32[]{:S(2)}, u32[]{:S(2)}) async-start(f32[16,72,128]{2,1,0:T(8,128)} %get-tuple-element.17), calls=%async_computation | async-start | bytes 1179648 | tf_op jit(solution)/shard_map/all_to_all | solution.py:512
  31.0 0.8 copy-start.1
  31.8 33.5 %all-to-all-start.1 = ((bf16[16,288,128]{2,1,0:T(8,128)(2,1)}), bf16[16,288,128]{2,1,0:T(8,128)(2,1)S(1)}, u32[]{:S(2)}, u32[]{:S(2)}) async-start(bf16[16,288,128]{2,1,0:T(8,128)(2,1)} %get-tuple-element.21), calls=%async_computation.1 | async-start | bytes 2359296 | tf_op jit(solution)/shard_map/all_to_all | solution.py:537
  35.4 29.9 %copy-start = (f32[1,8,64,1024]{3,2,1,0:T(8,128)S(1)}, f32[1,8,64,1024]{3,2,1,0:T(8,128)}, u32[]{:S(2)}) copy-start(f32[1,8,64,1024]{3,2,1,0:T(8,128)} %param.11) | copy-start | bytes 6291460

commit v4 on v3

--- a/solution.py
+++ b/solution.py
@@ -538,9 +538,20 @@
     incoming = pltpu.with_memory_space_constraint(incoming, pltpu.VMEM)
     far, weighted, model = call_model(sky, everyone, own)
     drive, squares = call_gradient(
-        band, block, far, weighted, pltpu.with_memory_space_constraint(vis, pltpu.VMEM), flag_mask, incoming, model, own, duals, consensus
+        band,
+        block,
+        far,
+        weighted,
+        pltpu.with_memory_space_constraint(vis, pltpu.VMEM),
+        pltpu.with_memory_space_constraint(flag_mask, pltpu.VMEM),
+        incoming,
+        model,
+        own,
+        duals,
+        consensus,
     )
     squares = lax.all_to_all(squares, "stn", 0, 0, tiled=True)
+    squares = pltpu.with_memory_space_constraint(squares, pltpu.VMEM)
     jones_next, shared = pl.pallas_call(
         update_kernel,
         out_shape=[shape((8, DIRS, OWN), F32), shape((BANDS, 64, 128), F32)],
@@ -549,6 +560,7 @@
         name="update",
     )(squares, drive, own, duals)
     gathered = lax.all_to_all(shared, "freq", 0, 0, tiled=True)
+    gathered = pltpu.with_memory_space_constraint(gathered, pltpu.VMEM)
     duals_next, consensus_next = pl.pallas_call(
         finish_kernel,
         grid=(1,),

time: 113 us -> 113 us (level)
  transfers between devices with their start and end apart: 2 -> 2, of which waited for: 2 -> 2; matrix products, arithmetic and copies ran while one was open for 0% -> 0% of each run, Pallas kernels for 28% -> 29%
where the time goes in v4:
time: 113 us; the launch traced here: 112 us
  Pallas kernels  52.7 us (47%)
  blocking collectives  27.9 us (25%)
  waiting for transfers between devices  16.5 us (15%)
  starting transfers between devices  13.6 us (12%)
    pallas_call x1, Pallas kernels, call_model(): pl.pallas_call(model_kernel, grid=(STEPS,), in_specs=[pl.BlockSpec((SPAN,...  24.5 us
    all_to_all x1, blocking collectives, local(): gathered = lax.all_to_all(shared, 'freq', 0, 0, tiled=True)  17.2 us
    pallas_call x1, Pallas kernels, call_gradient(): pl.pallas_call(gradient_kernel, grid=(STEPS,), in_specs=[SMEM, SMEM, pl.B...  15.3 us
    all_to_all x1, waiting for transfers between devices, local(): everyone = lax.all_to_all(copies, 'stn', 0, 0, tiled=True)  11.2 us
    all_to_all x1, blocking collectives, local(): squares = lax.all_to_all(squares, 'stn', 0, 0, tiled=True)  10.6 us
    all_to_all x1, starting transfers between devices, local(): everyone = lax.all_to_all(copies, 'stn', 0, 0, tiled=True)  9.98 us
    pallas_call x1, Pallas kernels, local(): pl.pallas_call(prepare_kernel, grid=(8,), in_specs=[SMEM, pl.BlockSpec((8...  7.47 us
    all_to_all x1, waiting for transfers between devices, local(): incoming = lax.all_to_all(outgoing, 'stn', 0, 0, tiled=True)  5.35 us
  transfers between devices with their start and end apart: 2, of which 2 were waited for; matrix products, arithmetic and copies ran while one was open for 0% of the time, Pallas kernels for 29%

profile of v4, /device:TPU:1, one launch (start us, length us, event | category | flops | bytes accessed | tf_op | source)
XLA Modules:
  0.0 112.2 jit_solution(11424997252783708533)
XLA Ops:
  0.6 1.8 %packet.1 = (f32[72,128]{1,0:T(8,128)}, f32[16,72,128]{2,1,0:T(8,128)}) custom-call(f32[8,16,64]{2,1,0:T(8,128)} %bitcast.19, f32[3,64]{1,0:T(4,128)} %stations_ref.1), custom_call_target="tpu_custom_call" | custom-call | tf_op jit(solution)/shard_map/packet/pallas_call | solution.py:505
  2.4 10.0 %all-to-all-start = ((f32[16,72,128]{2,1,0:T(8,128)}), f32[16,72,128]{2,1,0:T(8,128)S(1)}, u32[]{:S(2)}, u32[]{:S(2)}) async-start(f32[16,72,128]{2,1,0:T(8,128)} %get-tuple-element.17), calls=%async_computation | async-start | bytes 1179648 | tf_op jit(solution)/shard_map/all_to_all | solution.py:512
  12.4 7.5 %prepare.1 = (bf16[16,288,128]{2,1,0:T(8,128)(2,1)}, bf16[1536,128]{1,0:T(8,128)(2,1)}) custom-call(s32[1]{0:T(128)} %bitcast.band_ref, f32[8,64,1024]{2,1,0:T(8,128)} %bitcast.14, s32[64,1024]{1,0:T(8,128)} %mask_ref.3, f32[2,1536]{1,0:T(2,128)} %dirs_ref.1, f32[12,128]{1,0:T(8,128)} %bitcast.23, f32[2,1536]{1,0:T(2,128)} %pol_ref.1, f32[12,128]{1,0:T(8,128)} %bitcast.24, ...), custom_call_target="tpu_custom_call" | custom-call | flops 4000000000 | bytes 1000000 | tf_op jit(solution)/shard_map/prepare/pallas_call | solution.py:513
  19.9 11.2 %all-to-all-done.all_ref = f32[16,72,128]{2,1,0:T(8,128)S(1)} async-done(((f32[16,72,128]{2,1,0:T(8,128)}), f32[16,72,128]{2,1,0:T(8,128)S(1)}, u32[]{:S(2)}, u32[]{:S(2)}) %all-to-all-start) | async-done | bytes 589856 | tf_op jit(solution)/shard_map/all_to_all | solution.py:512
  31.0 0.0 copy-start.2
  31.0 0.8 copy-done.2
  31.8 3.6 %all-to-all-start.1 = ((bf16[16,288,128]{2,1,0:T(8,128)(2,1)}), bf16[16,288,128]{2,1,0:T(8,128)(2,1)S(1)}, u32[]{:S(2)}, u32[]{:S(2)}) async-start(bf16[16,288,128]{2,1,0:T(8,128)(2,1)} %get-tuple-element.21), calls=%async_computation.1 | async-start | bytes 2359296 | tf_op jit(solution)/shard_map/all_to_all | solution.py:537
  35.4 0.0 copy-start
  35.5 0.0 copy-start.1
  35.5 24.5 %model.1 = (bf16[4,1536,2048]{2,1,0:T(8,128)(2,1)}, bf16[6,1536,128]{2,1,0:T(8,128)(2,1)}, f32[256,2048]{1,0:T(8,128)}) custom-call(bf16[1536,128]{1,0:T(8,128)(2,1)} %get-tuple-element.16.sky_ref, f32[16,72,128]{2,1,0:T(8,128)} %copy-done.2, f32[72,128]{1,0:T(8,128)} %get-tuple-element.18.own_ref), custom_call_target="tpu_custom_call" | custom-call | flops 20000000000 | bytes 40000000 | tf_op jit(solution)/shard_map/model/pallas_call | solution.py:435
  60.0 5.4 %all-to-all-done.1.got_ref = bf16[16,288,128]{2,1,0:T(8,128)(2,1)S(1)} async-done(((bf16[16,288,128]{2,1,0:T(8,128)(2,1)}), bf16[16,288,128]{2,1,0:T(8,128)(2,1)S(1)}, u32[]{:S(2)}, u32[]{:S(2)}) %all-to-all-start.1) | async-done | bytes 1179680 | tf_op jit(solution)/shard_map/all_to_all | solution.py:537
  65.4 0.0 copy-done
  65.4 0.0 copy-done.1
  65.4 15.3 %gradient.1 = (f32[64,128]{1,0:T(8,128)}, f32[16,128]{1,0:T(8,128)}) custom-call(s32[1]{0:T(128)} %bitcast.band_ref, s32[1]{0:T(128)} %bitcast.1.block_ref, bf16[4,1536,2048]{2,1,0:T(8,128)(2,1)} %get-tuple-element.19.far_ref, bf16[6,1536,128]{2,1,0:T(8,128)(2,1)} %get-tuple-element.20.weighted_ref, f32[8,64,1024]{2,1,0:T(8,128)S(1)} %bitcast.15, ...), custom_call_target="tpu_custom_call" | custom-call | flops 7000000000 | bytes 30000000 | tf_op jit(solution)/shard_map/gradient/pallas_call | solution.py:465
  80.7 10.6 %all_to_all.26 = f32[16,1,128]{2,1,0:T(1,128)S(1)} all-to-all(f32[16,1,128]{2,1,0:T(1,128)} %bitcast.20), channel_id=1, replica_groups=mesh['freq'=16,'stn'=16] {'stn'}, dimensions={0} | all-to-all | bytes 16384 | tf_op jit(solution)/shard_map/all_to_all | solution.py:553
  91.3 1.9 %update.1 = (f32[8,16,64]{2,1,0:T(8,128)}, f32[16,64,128]{2,1,0:T(8,128)}) custom-call(f32[16,128]{1,0:T(8,128)S(1)} %bitcast.16, f32[64,128]{1,0:T(8,128)} %get-tuple-element.24.drive_ref, f32[72,128]{1,0:T(8,128)} %get-tuple-element.18.own_ref, f32[8,16,64]{2,1,0:T(8,128)} %bitcast.18), custom_call_target="tpu_custom_call" | custom-call | tf_op jit(solution)/shard_map/update/pallas_call | solution.py:555
  93.2 17.2 %all_to_all.27.shared_ref = f32[16,64,128]{2,1,0:T(8,128)S(1)} all-to-all(f32[16,64,128]{2,1,0:T(8,128)} %get-tuple-element.26.own_ref), channel_id=1, replica_groups=mesh['freq'=16,'stn'=16] {'freq'}, dimensions={0} | all-to-all | bytes 1048576 | tf_op jit(solution)/shard_map/all_to_all | solution.py:562
  110.4 1.7 %finish.1 = (f32[8,16,64]{2,1,0:T(8,128)}, f32[4,8,16,64]{3,2,1,0:T(8,128)}) custom-call(s32[1]{0:T(128)} %bitcast.band_ref, f32[16,64,128]{2,1,0:T(8,128)S(1)} %all_to_all.27.shared_ref, f32[16,64,128]{2,1,0:T(8,128)} %get-tuple-element.26.own_ref), custom_call_target="tpu_custom_call" | custom-call | tf_op jit(solution)/shard_map/finish/pallas_call | solution.py:564
Async XLA Ops:
  2.4 28.6 %all-to-all-start = ((f32[16,72,128]{2,1,0:T(8,128)}), f32[16,72,128]{2,1,0:T(8,128)S(1)}, u32[]{:S(2)}, u32[]{:S(2)}) async-start(f32[16,72,128]{2,1,0:T(8,128)} %get-tuple-element.17), calls=%async_computation | async-start | bytes 1179648 | tf_op jit(solution)/shard_map/all_to_all | solution.py:512
  31.0 0.8 copy-start.2
  31.8 33.5 %all-to-all-start.1 = ((bf16[16,288,128]{2,1,0:T(8,128)(2,1)}), bf16[16,288,128]{2,1,0:T(8,128)(2,1)S(1)}, u32[]{:S(2)}, u32[]{:S(2)}) async-start(bf16[16,288,128]{2,1,0:T(8,128)(2,1)} %get-tuple-element.21), calls=%async_computation.1 | async-start | bytes 2359296 | tf_op jit(solution)/shard_map/all_to_all | solution.py:537
  35.4 29.9 %copy-start = (f32[1,8,64,1024]{3,2,1,0:T(8,128)S(1)}, f32[1,8,64,1024]{3,2,1,0:T(8,128)}, u32[]{:S(2)}) copy-start(f32[1,8,64,1024]{3,2,1,0:T(8,128)} %param.11) | copy-start | bytes 6291460
  35.5 29.9 %copy-start.1 = (s32[64,1024]{1,0:T(8,128)S(1)}, s32[64,1024]{1,0:T(8,128)}, u32[]{:S(2)}) copy-start(s32[64,1024]{1,0:T(8,128)} %mask_ref.3) | copy-start | bytes 786436

commit v5 on v4

--- a/solution.py
+++ b/solution.py
@@ -19,7 +19,7 @@
 STEP_SIZE = 0.5
 F32 = jnp.float32
 BF16 = jnp.bfloat16
-SPAN = 384
+SPAN = 512
 CHUNK = 256
 STEPS = COMPS // SPAN
 VMEM = pl.BlockSpec(memory_space=pltpu.VMEM)

time: 113 us -> 113 us (level)
  transfers between devices with their start and end apart: 2 -> 2, of which waited for: 2 -> 2; matrix products, arithmetic and copies ran while one was open for 0% -> 0% of each run, Pallas kernels for 29% -> 28%
where the time goes in v5:
time: 113 us; the launch traced here: 112 us
  Pallas kernels  52.4 us (46%)
  blocking collectives  27.9 us (25%)
  waiting for transfers between devices  17 us (15%)
  starting transfers between devices  13.6 us (12%)
    pallas_call x1, Pallas kernels, call_model(): pl.pallas_call(model_kernel, grid=(STEPS,), in_specs=[pl.BlockSpec((SPAN,...  24.1 us
    all_to_all x1, blocking collectives, local(): gathered = lax.all_to_all(shared, 'freq', 0, 0, tiled=True)  17.2 us
    pallas_call x1, Pallas kernels, call_gradient(): pl.pallas_call(gradient_kernel, grid=(STEPS,), in_specs=[SMEM, SMEM, pl.B...  15.5 us
    all_to_all x1, waiting for transfers between devices, local(): everyone = lax.all_to_all(copies, 'stn', 0, 0, tiled=True)  11.2 us
    all_to_all x1, blocking collectives, local(): squares = lax.all_to_all(squares, 'stn', 0, 0, tiled=True)  10.6 us
    all_to_all x1, starting transfers between devices, local(): everyone = lax.all_to_all(copies, 'stn', 0, 0, tiled=True)  9.98 us
    pallas_call x1, Pallas kernels, local(): pl.pallas_call(prepare_kernel, grid=(8,), in_specs=[SMEM, pl.BlockSpec((8...  7.47 us
    all_to_all x1, waiting for transfers between devices, local(): incoming = lax.all_to_all(outgoing, 'stn', 0, 0, tiled=True)  5.82 us
  transfers between devices with their start and end apart: 2, of which 2 were waited for; matrix products, arithmetic and copies ran while one was open for 0% of the time, Pallas kernels for 28%

profile of v5, /device:TPU:1, one launch (start us, length us, event | category | flops | bytes accessed | tf_op | source)
XLA Modules:
  0.0 112.4 jit_solution(9183430376783376086)
XLA Ops:
  0.6 1.8 %packet.1 = (f32[72,128]{1,0:T(8,128)}, f32[16,72,128]{2,1,0:T(8,128)}) custom-call(f32[8,16,64]{2,1,0:T(8,128)} %bitcast.19, f32[3,64]{1,0:T(4,128)} %stations_ref.1), custom_call_target="tpu_custom_call" | custom-call | tf_op jit(solution)/shard_map/packet/pallas_call | solution.py:505
  2.4 10.0 %all-to-all-start = ((f32[16,72,128]{2,1,0:T(8,128)}), f32[16,72,128]{2,1,0:T(8,128)S(1)}, u32[]{:S(2)}, u32[]{:S(2)}) async-start(f32[16,72,128]{2,1,0:T(8,128)} %get-tuple-element.17), calls=%async_computation | async-start | bytes 1179648 | tf_op jit(solution)/shard_map/all_to_all | solution.py:512
  12.4 7.5 %prepare.1 = (bf16[16,288,128]{2,1,0:T(8,128)(2,1)}, bf16[1536,128]{1,0:T(8,128)(2,1)}) custom-call(s32[1]{0:T(128)} %bitcast.band_ref, f32[8,64,1024]{2,1,0:T(8,128)} %bitcast.14, s32[64,1024]{1,0:T(8,128)} %mask_ref.3, f32[2,1536]{1,0:T(2,128)} %dirs_ref.1, f32[12,128]{1,0:T(8,128)} %bitcast.23, f32[2,1536]{1,0:T(2,128)} %pol_ref.1, f32[12,128]{1,0:T(8,128)} %bitcast.24, ...), custom_call_target="tpu_custom_call" | custom-call | flops 4000000000 | bytes 1000000 | tf_op jit(solution)/shard_map/prepare/pallas_call | solution.py:513
  19.9 11.2 %all-to-all-done.all_ref = f32[16,72,128]{2,1,0:T(8,128)S(1)} async-done(((f32[16,72,128]{2,1,0:T(8,128)}), f32[16,72,128]{2,1,0:T(8,128)S(1)}, u32[]{:S(2)}, u32[]{:S(2)}) %all-to-all-start) | async-done | bytes 589856 | tf_op jit(solution)/shard_map/all_to_all | solution.py:512
  31.0 0.0 copy-start.2
  31.0 0.8 copy-done.2
  31.8 3.6 %all-to-all-start.1 = ((bf16[16,288,128]{2,1,0:T(8,128)(2,1)}), bf16[16,288,128]{2,1,0:T(8,128)(2,1)S(1)}, u32[]{:S(2)}, u32[]{:S(2)}) async-start(bf16[16,288,128]{2,1,0:T(8,128)(2,1)} %get-tuple-element.21), calls=%async_computation.1 | async-start | bytes 2359296 | tf_op jit(solution)/shard_map/all_to_all | solution.py:537
  35.4 0.0 copy-start
  35.5 0.0 copy-start.1
  35.5 24.1 %model.1 = (bf16[4,1536,2048]{2,1,0:T(8,128)(2,1)}, bf16[6,1536,128]{2,1,0:T(8,128)(2,1)}, f32[256,2048]{1,0:T(8,128)}) custom-call(bf16[1536,128]{1,0:T(8,128)(2,1)} %get-tuple-element.16.sky_ref, f32[16,72,128]{2,1,0:T(8,128)} %copy-done.2, f32[72,128]{1,0:T(8,128)} %get-tuple-element.18.own_ref), custom_call_target="tpu_custom_call" | custom-call | flops 20000000000 | bytes 40000000 | tf_op jit(solution)/shard_map/model/pallas_call | solution.py:435
  59.6 5.8 %all-to-all-done.1.got_ref = bf16[16,288,128]{2,1,0:T(8,128)(2,1)S(1)} async-done(((bf16[16,288,128]{2,1,0:T(8,128)(2,1)}), bf16[16,288,128]{2,1,0:T(8,128)(2,1)S(1)}, u32[]{:S(2)}, u32[]{:S(2)}) %all-to-all-start.1) | async-done | bytes 1179680 | tf_op jit(solution)/shard_map/all_to_all | solution.py:537
  65.4 0.0 copy-done
  65.4 0.0 copy-done.1
  65.4 15.5 %gradient.1 = (f32[64,128]{1,0:T(8,128)}, f32[16,128]{1,0:T(8,128)}) custom-call(s32[1]{0:T(128)} %bitcast.band_ref, s32[1]{0:T(128)} %bitcast.1.block_ref, bf16[4,1536,2048]{2,1,0:T(8,128)(2,1)} %get-tuple-element.19.far_ref, bf16[6,1536,128]{2,1,0:T(8,128)(2,1)} %get-tuple-element.20.weighted_ref, f32[8,64,1024]{2,1,0:T(8,128)S(1)} %bitcast.15, ...), custom_call_target="tpu_custom_call" | custom-call | flops 7000000000 | bytes 30000000 | tf_op jit(solution)/shard_map/gradient/pallas_call | solution.py:465
  80.9 10.6 %all_to_all.26 = f32[16,1,128]{2,1,0:T(1,128)S(1)} all-to-all(f32[16,1,128]{2,1,0:T(1,128)} %bitcast.20), channel_id=1, replica_groups=mesh['freq'=16,'stn'=16] {'stn'}, dimensions={0} | all-to-all | bytes 16384 | tf_op jit(solution)/shard_map/all_to_all | solution.py:553
  91.5 1.9 %update.1 = (f32[8,16,64]{2,1,0:T(8,128)}, f32[16,64,128]{2,1,0:T(8,128)}) custom-call(f32[16,128]{1,0:T(8,128)S(1)} %bitcast.16, f32[64,128]{1,0:T(8,128)} %get-tuple-element.24.drive_ref, f32[72,128]{1,0:T(8,128)} %get-tuple-element.18.own_ref, f32[8,16,64]{2,1,0:T(8,128)} %bitcast.18), custom_call_target="tpu_custom_call" | custom-call | tf_op jit(solution)/shard_map/update/pallas_call | solution.py:555
  93.4 17.2 %all_to_all.27.shared_ref = f32[16,64,128]{2,1,0:T(8,128)S(1)} all-to-all(f32[16,64,128]{2,1,0:T(8,128)} %get-tuple-element.26.own_ref), channel_id=1, replica_groups=mesh['freq'=16,'stn'=16] {'freq'}, dimensions={0} | all-to-all | bytes 1048576 | tf_op jit(solution)/shard_map/all_to_all | solution.py:562
  110.7 1.7 %finish.1 = (f32[8,16,64]{2,1,0:T(8,128)}, f32[4,8,16,64]{3,2,1,0:T(8,128)}) custom-call(s32[1]{0:T(128)} %bitcast.band_ref, f32[16,64,128]{2,1,0:T(8,128)S(1)} %all_to_all.27.shared_ref, f32[16,64,128]{2,1,0:T(8,128)} %get-tuple-element.26.own_ref), custom_call_target="tpu_custom_call" | custom-call | tf_op jit(solution)/shard_map/finish/pallas_call | solution.py:564
Async XLA Ops:
  2.4 28.6 %all-to-all-start = ((f32[16,72,128]{2,1,0:T(8,128)}), f32[16,72,128]{2,1,0:T(8,128)S(1)}, u32[]{:S(2)}, u32[]{:S(2)}) async-start(f32[16,72,128]{2,1,0:T(8,128)} %get-tuple-element.17), calls=%async_computation | async-start | bytes 1179648 | tf_op jit(solution)/shard_map/all_to_all | solution.py:512
  31.0 0.8 copy-start.2
  31.8 33.5 %all-to-all-start.1 = ((bf16[16,288,128]{2,1,0:T(8,128)(2,1)}), bf16[16,288,128]{2,1,0:T(8,128)(2,1)S(1)}, u32[]{:S(2)}, u32[]{:S(2)}) async-start(bf16[16,288,128]{2,1,0:T(8,128)(2,1)} %get-tuple-element.21), calls=%async_computation.1 | async-start | bytes 2359296 | tf_op jit(solution)/shard_map/all_to_all | solution.py:537
  35.4 29.9 %copy-start = (f32[1,8,64,1024]{3,2,1,0:T(8,128)S(1)}, f32[1,8,64,1024]{3,2,1,0:T(8,128)}, u32[]{:S(2)}) copy-start(f32[1,8,64,1024]{3,2,1,0:T(8,128)} %param.11) | copy-start | bytes 6291460
  35.5 29.9 %copy-start.1 = (s32[64,1024]{1,0:T(8,128)S(1)}, s32[64,1024]{1,0:T(8,128)}, u32[]{:S(2)}) copy-start(s32[64,1024]{1,0:T(8,128)} %mask_ref.3) | copy-start | bytes 786436
